TPU v7x, 32 devices: a whole 2x2x4 slice. The times are simulated.
32 devices in a mesh: bucket: 8 (over z, x), entity: 4 (over y, core).
Axes of the slice: x: 2, y: 2, z: 4, core: 2. Of those that a mesh axis runs over, the one named last changes fastest.
Arguments:
- ent_table: bfloat16 [4096, 512], P('entity'), may hold values from -0.25 to 0.25
- panels: bfloat16 [32, 512, 512], P(('bucket', 'entity')), may hold values from -0.25 to 0.25
- rel_vecs: bfloat16 [32, 512], P(('bucket', 'entity')), may hold values from -0.19921875 to 0.19921875
- head_slots: int32 [32, 2, 128], P(('bucket', 'entity')), may hold values from 0 to 63
- tail_slots: int32 [32, 2, 128], P(('bucket', 'entity')), may hold values from 0 to 63
- negatives: int32 [32, 2, 512], P(('bucket', 'entity')), may hold values from 0 to 63
- requests: int32 [32, 4, 16], P(('bucket', 'entity')), may hold values from 0 to 1023, as said below
- block_count: int32 [32], P(('bucket', 'entity')), may hold values from 1 to 2, as said below
Outputs:
- ent_grad: float32 [4096, 512], P('entity', 'bucket')
- panel_grad: float32 [32, 512, 512], P(('bucket', 'entity'))
- rel_grad: float32 [32, 512], P(('bucket', 'entity'))
Inputs may be any that keep to these rules, and one draw needn't show every extreme that they name: `requests`: for each device and row shard the 16 row numbers are distinct. `block_count`: at least one device has exactly 2 live blocks.
All inputs are finite; a program needn't handle non-finite values.
Results may differ from a plain program's by a relative error of at most 0.0095.
Values may be sent and summed in bfloat16 or wider, within the bound.
No kernel may reach another device: no remote copies, remote signals or barrier semaphores. Data moves between devices by JAX's collectives and lax.ppermute only.
A program may use at most 64 MiB of HBM per device.

v0:
```python
import jax
import jax.numpy as jnp
from jax import lax
from jax.sharding import PartitionSpec as P

NEG = 512


MARGIN = 2.0


def block_terms(projected, grad_start, relation, head_one, tail_one, cand_one, live_mask):
    feature_count = projected.shape[1]
    head_rows = jnp.take(projected, head_one, axis=0)
    tail_rows = jnp.take(projected, tail_one, axis=0)
    cand_rows = jnp.take(projected, cand_one, axis=0)
    centers = (head_rows.astype(jnp.float32) + relation).astype(jnp.bfloat16)
    center_f = centers.astype(jnp.float32)
    offset = center_f - tail_rows.astype(jnp.float32)
    pos_dist = jnp.sum(offset * offset, -1)
    pos_weight = jax.nn.sigmoid(pos_dist - MARGIN) * live_mask[:, None]
    cross_terms = jnp.einsum("bed,bnd->ben", centers, cand_rows, preferred_element_type=jnp.float32)
    cand_square = jnp.sum(jnp.square(cand_rows.astype(jnp.float32)), -1)
    neg_dist = (
        jnp.sum(center_f * center_f, -1)[:, :, None] + cand_square[:, None, :] - 2.0 * cross_terms
    )
    neg_weight = -jax.nn.sigmoid(MARGIN - neg_dist) / NEG * live_mask[:, None, None]
    weight_b = neg_weight.astype(jnp.bfloat16)
    grad_center = (
        2.0 * pos_weight[..., None] * offset
        + 2.0 * jnp.sum(neg_weight, -1)[..., None] * center_f
        - 2.0 * jnp.einsum("ben,bnd->bed", weight_b, cand_rows, preferred_element_type=jnp.float32)
    )
    grad_tail = -2.0 * pos_weight[..., None] * offset
    grad_cand = 2.0 * jnp.sum(neg_weight, 1)[..., None] * cand_rows.astype(
        jnp.float32
    ) - 2.0 * jnp.einsum("ben,bed->bnd", weight_b, centers, preferred_element_type=jnp.float32)
    grad_proj = grad_start.at[head_one.reshape(-1)].add(grad_center.reshape(-1, feature_count))
    grad_proj = grad_proj.at[tail_one.reshape(-1)].add(grad_tail.reshape(-1, feature_count))
    grad_proj = grad_proj.at[cand_one.reshape(-1)].add(grad_cand.reshape(-1, feature_count))
    return (grad_proj, jnp.sum(grad_center, (0, 1)))


def body(ent_table, panels, rel_vecs, head_slots, tail_slots, negatives, requests, block_count):
    shard_count = lax.axis_size("entity")
    feature_count = ent_table.shape[1]
    asked = lax.all_to_all(requests[0], "entity", split_axis=0, concat_axis=0, tiled=True)
    found = jnp.take(ent_table, asked, axis=0)
    returned = lax.all_to_all(found, "entity", split_axis=0, concat_axis=0, tiled=True)
    fetched = returned
    fetched = fetched.reshape(-1, feature_count)
    rel_panel = panels[0]
    projected = jnp.dot(fetched, rel_panel.T, preferred_element_type=jnp.float32).astype(
        jnp.bfloat16
    )
    relation = rel_vecs[0].astype(jnp.float32)
    slot_total = head_slots.shape[1]
    grad_empty = jnp.zeros(projected.shape, jnp.float32)
    live_mask = (jnp.arange(slot_total) < block_count[0]).astype(jnp.float32)
    grad_proj, grad_rel = block_terms(
        projected, grad_empty, relation, head_slots[0], tail_slots[0], negatives[0], live_mask
    )
    grad_proj_b = grad_proj.astype(jnp.bfloat16)
    grad_fetched = jnp.dot(grad_proj_b, rel_panel, preferred_element_type=jnp.float32)
    grad_panel = jnp.einsum("kd,ke->de", grad_proj_b, fetched, preferred_element_type=jnp.float32)
    shard_rows = ent_table.shape[0]
    cap_rows = asked.shape[1]
    outgoing = grad_fetched.reshape(shard_count, cap_rows, feature_count)
    incoming = lax.all_to_all(outgoing, "entity", split_axis=0, concat_axis=0, tiled=True)
    shard_grad = jnp.zeros((shard_rows, feature_count), jnp.float32)
    shard_grad = shard_grad.at[asked.reshape(-1)].add(incoming.reshape(-1, feature_count))
    ent_part = lax.psum_scatter(shard_grad, "bucket", scatter_dimension=1, tiled=True)
    return (ent_part, grad_panel[None], grad_rel[None])


def solution(mesh):
    placed = (
        P("entity", None),
        P(("bucket", "entity"), None, None),
        P(("bucket", "entity"), None),
        P(("bucket", "entity"), None, None),
        P(("bucket", "entity"), None, None),
        P(("bucket", "entity"), None, None),
        P(("bucket", "entity"), None, None),
        P(("bucket", "entity")),
    )
    return jax.shard_map(
        body,
        mesh=mesh,
        in_specs=placed,
        out_specs=(
            P("entity", "bucket"),
            P(("bucket", "entity"), None, None),
            P(("bucket", "entity"), None),
        ),
        check_vma=False,
    )
```

profile of v0, /device:TPU:0, one launch (start us, length us, event | category | flops | bytes accessed | tf_op | source)
XLA Modules:
  0.0 141.9 jit_solution(12106276101897012541)
XLA Ops:
  7.2 4.4 %all-to-all-start = ((s32[4,1,16]{2,1,0:T(1,128)}), s32[4,1,16]{2,1,0:T(1,128)S(1)}, u32[]{:S(2)}, u32[]{:S(2)}) async-start(s32[4,1,16]{2,1,0:T(1,128)} %bitcast.108), calls=%async_computation | async-start | bytes 4096 | tf_op jit(solution)/shard_map/all_to_all | solution.py:47
  11.6 0.7 fusion.27
  12.2 0.7 compare_and_fusion
  12.9 0.7 fusion.29
  13.6 0.7 compare_and_fusion.1
  14.3 0.7 fusion.30
  15.0 0.7 compare_select_fusion.4
  16.4 0.7 compare_select_fusion.3
  17.1 0.7 copy.22
  17.9 0.7 gather_fusion
  18.6 0.7 broadcast_select_fusion.4
  19.3 3.3 %all-to-all-start.1 = ((bf16[4,16,512]{2,1,0:T(8,128)(2,1)}), bf16[4,16,512]{2,1,0:T(8,128)(2,1)S(1)}, u32[]{:S(2)}, u32[]{:S(2)}) async-start(bf16[4,16,512]{2,1,0:T(8,128)(2,1)} %broadcast_select_fusion.4), calls=%async_computation.1 | async-start | bytes 131072 | tf_op jit(solution)/shard_map/all_to_all | solution.py:49
  22.6 0.7 convert_element_type.57
  24.6 2.2 %all-to-all-done.1 = bf16[4,16,512]{2,1,0:T(8,128)(2,1)S(1)} async-done(((bf16[4,16,512]{2,1,0:T(8,128)(2,1)}), bf16[4,16,512]{2,1,0:T(8,128)(2,1)S(1)}, u32[]{:S(2)}, u32[]{:S(2)}) %all-to-all-start.1) | async-done | bytes 65568 | tf_op jit(solution)/shard_map/all_to_all | solution.py:49
  26.7 1.3 convolution_convert_fusion
  28.1 4.0 %gather_fusion.1 = bf16[1024,512]{1,0:T(8,128)(2,1)S(1)} fusion(bf16[64,512]{1,0:T(8,128)(2,1)S(1)} %convolution_convert_fusion, s32[1024]{0:T(1024)S(1)} %broadcast_clamp_fusion), kind=kCustom, calls=%fused_computation.3 | custom fusion | bytes 2101248 | tf_op jit(solution)/shard_map/jit(_take)/gather | solution.py:16
  32.0 1.2 gather_fusion.2
  34.1 1.4 fusion.33
  35.5 1.2 gather_fusion.3
  37.0 1.0 fusion.22
  38.0 2.0 %fusion.2 = f32[2,512,512]{2,1,0:T(8,128)} fusion(f32[2,512]{1,0:T(2,128)S(1)} %broadcast_multiply_fusion, bf16[2,512,512]{2,1,0:T(8,128)(2,1)S(1)} %bitcast.77, pred[2,512]{1,0:T(4,128)(4,1)S(1)} %compare_and_fusion, bf16[2,128,512]{2,1,0:T(8,128)(2,1)S(1)} %copy-done.2, bf16[2,128,512]{2,1,0:T(8,128)(2,1)S(1)} %bitcast.82, f32[512]{0:T(512)S(1)} %bitcast.100, ...), kind=kOutput, calls=%fused_computation.12 | convolution fusion | flops 137363456 | bytes 3677440 | tf_op jit(solution)/shard_map/ben,bed->bnd/dot_general | solution.py:37
  40.0 1.1 fusion.34
  41.1 2.1 %scatter_custom_fusion = f32[64,512]{1,0:T(8,128)S(1)} fusion(s32[256]{0:T(256)S(1)} %bitcast.109, f32[256,512]{1,0:T(8,128)S(1)} %bitcast.110, f32[]{:T(128)} %constant.19.clone.1), kind=kCustom, calls=%fused_computation.46 | custom fusion | flops 131072 | bytes 131076 | tf_op jit(solution)/shard_map/scatter-add | solution.py:38
  43.3 2.8 %scatter_fusion = f32[64,512]{1,0:T(8,128)S(1)} fusion(f32[64,512]{1,0:T(8,128)S(1)} %scatter_custom_fusion, s32[256]{0:T(256)S(1)} %bitcast.107, f32[256,512]{1,0:T(8,128)} %bitcast.87), kind=kCustom, calls=%fused_computation.5 | custom fusion | flops 131072 | bytes 1573888 | tf_op jit(solution)/shard_map/scatter-add | solution.py:39
  46.1 6.7 %scatter_fusion.1 = f32[64,512]{1,0:T(8,128)S(1)} fusion(f32[64,512]{1,0:T(8,128)S(1)} %scatter_fusion, s32[1024]{0:T(1024)S(1)} %bitcast.102, f32[1024,512]{1,0:T(8,128)S(1)} %bitcast.86), kind=kCustom, calls=%fused_computation.6 | custom fusion | flops 524288 | bytes 6295552 | tf_op jit(solution)/shard_map/scatter-add | solution.py:40
  52.8 1.9 %fusion.17 = f32[4,16,512]{2,1,0:T(8,128)} fusion(bf16[4,16,512]{2,1,0:T(8,128)(2,1)S(1)} %bitcast.90, bf16[1,512,512]{2,1,0:T(8,128)(2,1)} %param.11), kind=kOutput, calls=%fused_computation.35 | convolution fusion | flops 33554432 | bytes 720896 | tf_op jit(solution)/shard_map/dot_general | solution.py:64
  54.7 3.3 %all-to-all-start.2 = ((f32[4,16,512]{2,1,0:T(8,128)}), f32[4,16,512]{2,1,0:T(8,128)S(1)}, u32[]{:S(2)}, u32[]{:S(2)}) async-start(f32[4,16,512]{2,1,0:T(8,128)} %fusion.17), calls=%async_computation.2 | async-start | bytes 262144 | tf_op jit(solution)/shard_map/all_to_all | solution.py:69
  58.1 4.5 %all-to-all-done.2 = f32[4,16,512]{2,1,0:T(8,128)S(1)} async-done(((f32[4,16,512]{2,1,0:T(8,128)}), f32[4,16,512]{2,1,0:T(8,128)S(1)}, u32[]{:S(2)}, u32[]{:S(2)}) %all-to-all-start.2) | async-done | bytes 131104 | tf_op jit(solution)/shard_map/all_to_all | solution.py:69
  62.6 1.5 %scatter_custom_fusion.3 = f32[1024,512]{1,0:T(8,128)S(1)} fusion(s32[64]{0:T(128)S(1)} %fusion.28, f32[64,512]{1,0:T(8,128)S(1)} %bitcast.92, f32[]{:T(128)} %constant.19.clone.1), kind=kCustom, calls=%fused_computation.27 | custom fusion | flops 32768 | bytes 2097156 | tf_op jit(solution)/shard_map/scatter-add | solution.py:71
  64.1 1.9 %copy.19 = f32[1024,512]{0,1:T(8,128)} copy(f32[1024,512]{1,0:T(8,128)S(1)} %scatter_custom_fusion.3) | data formatting | bytes 4194304
  66.0 1.3 convolution_bitcast_fusion
  67.3 67.8 %reduce-scatter.4.cloned.1.call-done = f32[64,1024]{1,0:T(8,128)} async-done(((f32[512,1024]{1,0:T(8,128)}), f32[64,1024]{1,0:T(8,128)}) %reduce-scatter.4.cloned.1.call-update) | async-done | bytes 262160
  (34 shorter events, 2.8 us)
Async XLA Ops:
  7.2 10.7 %copy-start = (bf16[1024,512]{1,0:T(8,128)(2,1)S(1)}, bf16[1024,512]{1,0:T(8,128)(2,1)}, u32[]{:S(2)}) copy-start(bf16[1024,512]{1,0:T(8,128)(2,1)} %param.10) | copy-start | bytes 3145732
  7.2 10.6 %all-to-all-start = ((s32[4,1,16]{2,1,0:T(1,128)}), s32[4,1,16]{2,1,0:T(1,128)S(1)}, u32[]{:S(2)}, u32[]{:S(2)}) async-start(s32[4,1,16]{2,1,0:T(1,128)} %bitcast.108), calls=%async_computation | async-start | bytes 4096 | tf_op jit(solution)/shard_map/all_to_all | solution.py:47
  19.3 7.4 %all-to-all-start.1 = ((bf16[4,16,512]{2,1,0:T(8,128)(2,1)}), bf16[4,16,512]{2,1,0:T(8,128)(2,1)S(1)}, u32[]{:S(2)}, u32[]{:S(2)}) async-start(bf16[4,16,512]{2,1,0:T(8,128)(2,1)} %broadcast_select_fusion.4), calls=%async_computation.1 | async-start | bytes 131072 | tf_op jit(solution)/shard_map/all_to_all | solution.py:49
  35.4 2.6 %copy-start.2 = (bf16[2,128,512]{2,1,0:T(8,128)(2,1)S(1)}, bf16[2,128,512]{2,1,0:T(8,128)(2,1)}, u32[]{:S(2)}) copy-start(bf16[2,128,512]{2,1,0:T(8,128)(2,1)} %get-tuple-element.14) | copy-start | bytes 786436
  38.0 2.0 %copy-start.3 = (bf16[2,128,512]{2,1,0:T(8,128)(2,1)S(1)}, bf16[2,128,512]{2,1,0:T(8,128)(2,1)}, u32[]{:S(2)}) copy-start(bf16[2,128,512]{2,1,0:T(8,128)(2,1)} %get-tuple-element.14) | copy-start | bytes 786436
  43.2 2.8 %copy-start.1 = (f32[2,512,512]{2,1,0:T(8,128)S(1)}, f32[2,512,512]{2,1,0:T(8,128)}, u32[]{:S(2)}) copy-start(f32[2,512,512]{2,1,0:T(8,128)} %fusion.2) | copy-start | bytes 6291460
  54.7 7.9 %all-to-all-start.2 = ((f32[4,16,512]{2,1,0:T(8,128)}), f32[4,16,512]{2,1,0:T(8,128)S(1)}, u32[]{:S(2)}, u32[]{:S(2)}) async-start(f32[4,16,512]{2,1,0:T(8,128)} %fusion.17), calls=%async_computation.2 | async-start | bytes 262144 | tf_op jit(solution)/shard_map/all_to_all | solution.py:69
  58.0 77.0 %reduce-scatter.4.cloned.1.call-start = ((), (), s32[]{:S(2)}) async-start(), calls=%async_computation.4 | async-start | bytes 2359296
Sparse Core Ops, SparseCore 0:
  66.1 68.9 reduce-scatter.3
where the time goes:
time: 143 us; the launch traced here: 142 us
  waiting for transfers between devices  74.5 us (52%)
  other arithmetic  22.3 us (16%)
  between operations  14.9 us (10%)
  starting transfers between devices  11 us (8%)
  local copies, waits for them, and re-layouts  10.2 us (7%)
  matrix products  8.99 us (6%)
    unnamed x2, waiting for transfers between devices  67.8 us
    scatter-add x1, other arithmetic, block_terms(): grad_proj.at[cand_one.reshape(-1)].add(grad_cand.reshape(-1, feature_count))  6.67 us
    all_to_all x1, waiting for transfers between devices, body(): lax.all_to_all(outgoing, 'entity', split_axis=0, concat_axis=0, tiled=True)  4.54 us
    all_to_all x1, starting transfers between devices, body(): lax.all_to_all(requests[0], 'entity', split_axis=0, concat_axis=0, tiled=...  4.38 us
    gather x1, local copies, waits for them, and re-layouts, block_terms(): cand_rows = jnp.take(projected, cand_one, axis=0)  3.96 us
    all_to_all x1, starting transfers between devices, body(): lax.all_to_all(outgoing, 'entity', split_axis=0, concat_axis=0, tiled=True)  3.33 us
    all_to_all x1, starting transfers between devices, body(): lax.all_to_all(found, 'entity', split_axis=0, concat_axis=0, tiled=True)  3.29 us
  transfers between devices with their start and end apart: 4, of which 3 were waited for; matrix products, arithmetic and copies ran while one was open for 6% of the time, Pallas kernels for 0%

commit v1 on v0

v1 whole, which is shorter than its diff:
```python
import jax
import jax.numpy as jnp
from jax import lax
from jax.experimental import pallas as pl
from jax.experimental.pallas import tpu as pltpu
from jax.sharding import PartitionSpec as P

MARGIN = 2.0
LANES = 128
DIGIT = 256
F32 = jnp.float32
BF16 = jnp.bfloat16
I32 = jnp.int32
VMEM_BYTES = 16 * 1024 * 1024


def dot(a, b, over):
    return lax.dot_general(a, b, ((over[:1], over[1:]), ((), ())), preferred_element_type=F32)


def iota(shape, axis):
    return lax.broadcasted_iota(I32, shape, axis)


def to_column(row_blocks):
    k = row_blocks[0].shape[1]
    tall = jnp.concatenate([jnp.broadcast_to(r, (k, k)) for r in row_blocks], axis=0)
    pick = lax.rem(iota(tall.shape, 0), k) == iota(tall.shape, 1)
    return jnp.sum(jnp.where(pick, tall, 0).astype(F32), axis=1, keepdims=True)


def flip(column):
    n = column.shape[0]
    return jnp.sum(jnp.where(iota((n, n), 0) == iota((n, n), 1), column, 0.0), axis=0, keepdims=True)


def flip_back(row):
    n = row.shape[1]
    return jnp.sum(jnp.where(iota((n, n), 0) == iota((n, n), 1), row, 0.0), axis=1, keepdims=True)


def call(kernel, outs, flops=0, nbytes=0):
    vmem = pl.BlockSpec(memory_space=pltpu.VMEM)
    smem = pl.BlockSpec(memory_space=pltpu.SMEM)

    def run(*args, scalars=()):
        return pl.pallas_call(
            kernel,
            out_shape=outs,
            in_specs=[smem] * len(scalars) + [vmem] * len(args),
            out_specs=[vmem] * len(outs),
            compiler_params=pltpu.CompilerParams(vmem_limit_bytes=VMEM_BYTES),
            cost_estimate=pl.CostEstimate(flops=flops, bytes_accessed=nbytes, transcendentals=0),
        )(*scalars, *args)

    return run


def counts_kernel(count_ref, head_ref, tail_ref, neg_ref, req_ref, edges_ref, pairs_ref, rows_ref):
    shards, cap = req_ref.shape[1:]
    total = shards * cap
    me = lax.axis_index("entity")
    blocks, edge = head_ref.shape[1:]
    negs = neg_ref.shape[2]
    live_blocks = count_ref[0]
    edges = jnp.zeros((total, total), F32)
    pairs = jnp.zeros((total, total), F32)
    edge_slot = jnp.bitwise_xor(iota((total, edge), 0), me * cap)
    neg_slot = jnp.bitwise_xor(iota((total, negs), 0), me * cap)
    for j in range(blocks):
        live = (j < live_blocks).astype(F32)
        head = (head_ref[0, j : j + 1, :] == edge_slot).astype(F32) * live
        tail = (tail_ref[0, j : j + 1, :] == edge_slot).astype(F32)
        neg = (neg_ref[0, j : j + 1, :] == neg_slot).astype(F32)
        edges += dot(head.astype(BF16), tail.astype(BF16), (1, 1))
        heads = jnp.sum(head, axis=1, keepdims=True)
        negatives = dot(jnp.ones((8, negs), BF16), neg.astype(BF16), (1, 1))[0:1]
        pairs += heads * negatives
    edges_ref[...] = edges
    pairs_ref[...] = pairs
    column = to_column([req_ref[0, pl.ds(jnp.bitwise_xor(me, s), 1), :] for s in range(shards)])
    high = jnp.floor(column * (1.0 / DIGIT))
    low = column - high * DIGIT
    rows_ref[...] = jnp.where(iota((total, LANES), 1) < 96, high, low)


def pick_kernel(*refs):
    table_ref, asked, outs = refs[0], refs[1 : 1 + (len(refs) - 1) // 2], refs[1 + (len(refs) - 1) // 2 :]
    me = lax.axis_index("entity")
    cap = asked[0].shape[2]
    column = to_column([r[0, pl.ds(me, 1), :] for r in asked]).astype(I32)
    rows = table_ref.shape[0]
    hot = (column == iota((column.shape[0], rows), 1)).astype(F32).astype(BF16)
    found = dot(hot, table_ref[...], (1, 0)).astype(BF16)
    for s, out in enumerate(outs):
        out[...] = found[s * cap : (s + 1) * cap]


def terms_kernel(buckets, negs, *refs):
    panel_ref, rel_ref, edges_ref, pairs_ref, rows_ref = refs[:5]
    send_ref, grad_ref, rel_grad_ref = refs[-3:]
    parts = refs[5:-3]
    shards = len(parts)
    fetched = jnp.concatenate([r[...] for r in parts], axis=0)
    panel = panel_ref[0]
    proj = dot(fetched, panel, (1, 1)).astype(BF16)
    proj_f = proj.astype(F32)
    centers = (proj_f + rel_ref[...].astype(F32)).astype(BF16)
    center_f = centers.astype(F32)
    cross = dot(centers, proj, (1, 1))
    dist = (
        jnp.sum(center_f * center_f, axis=1, keepdims=True)
        + flip(jnp.sum(proj_f * proj_f, axis=1, keepdims=True))
        - 2.0 * cross
    )
    pos = edges_ref[...] * jax.nn.sigmoid(dist - MARGIN)
    neg = -jax.nn.sigmoid(MARGIN - dist) * (1.0 / negs)
    exact = pos + pairs_ref[...] * neg
    rounded = pos + pairs_ref[...] * neg.astype(BF16).astype(F32)
    high = rounded.astype(BF16)
    low = (rounded - high.astype(F32)).astype(BF16)
    row_sum = jnp.sum(exact, axis=1, keepdims=True)
    col_sum = flip_back(jnp.sum(exact, axis=0, keepdims=True))
    grad_center = 2.0 * (row_sum * center_f - dot(high, proj, (1, 0)) - dot(low, proj, (1, 0)))
    grad_other = 2.0 * (col_sum * proj_f - dot(high, centers, (0, 0)) - dot(low, centers, (0, 0)))
    rel_grad_ref[...] = jnp.sum(grad_center, axis=0, keepdims=True)
    grad = (grad_center + grad_other).astype(BF16)
    grad_ref[...] = grad
    grad_rows = dot(grad, panel, (1, 0))
    total, features = grad_rows.shape
    cap = total // shards
    width = features // buckets
    me = lax.axis_index("entity")
    lane = iota((total, LANES), 1)
    for b in range(buckets):
        block, offset = divmod(b * width, LANES)
        piece = grad_rows[:, block * LANES : (block + 1) * LANES]
        if offset:
            piece = pltpu.roll(piece, LANES - offset, 1)
        piece = jnp.where(lane < width, piece, rows_ref[...]).astype(BF16)
        for s in range(shards):
            send_ref[b * shards + jnp.bitwise_xor(me, s)] = piece[s * cap : (s + 1) * cap]


def panel_kernel(grad_ref, *refs):
    fetched = jnp.concatenate([r[...] for r in refs[:-1]], axis=0)
    refs[-1][0] = dot(grad_ref[...], fetched, (0, 0))


def sum_kernel(width, got_ref, out_ref):
    devices, cap, _ = got_ref.shape
    rows = out_ref.shape[1]
    step = min(devices, 512 // cap)

    def part(i):
        got = got_ref[pl.ds(i * step, step)].reshape(step * cap, LANES)
        wide = got.astype(F32)
        column = (wide[:, 64:65] * DIGIT + wide[:, 96:97]).astype(I32)
        hot = (column == iota((step * cap, rows), 1)).astype(F32).astype(BF16)
        return dot(jnp.transpose(wide)[:width].astype(BF16), hot, (1, 0))

    if devices == step:
        out_ref[...] = part(0)
    else:
        out_ref[...] = jnp.zeros_like(out_ref)

        def add(i, _):
            out_ref[...] += part(i)
            return 0

        lax.fori_loop(0, devices // step, add, 0)


def body(ent_table, panels, rel_vecs, head_slots, tail_slots, negatives, requests, block_count):
    shards = lax.axis_size("entity")
    buckets = lax.axis_size("bucket")
    shard_rows, features = ent_table.shape
    cap = requests.shape[2]
    total = shards * cap
    width = features // buckets

    def swap(x, s):
        return lax.ppermute(x, "entity", [(i, i ^ s) for i in range(shards)])

    def out(shape, dtype=F32):
        return jax.ShapeDtypeStruct(shape, dtype)

    asked = [requests] + [swap(requests, s) for s in range(1, shards)]
    edges, pairs, rows = call(
        counts_kernel, [out((total, total)), out((total, total)), out((total, LANES))]
    )(head_slots, tail_slots, negatives, requests, scalars=(block_count,))
    found = call(pick_kernel, [out((cap, features), BF16)] * shards)(ent_table, *asked)
    parts = [found[0]] + [swap(found[s], s) for s in range(1, shards)]
    send, grad, rel_grad = call(
        lambda *refs: terms_kernel(buckets, negatives.shape[2], *refs),
        [out((buckets * shards, cap, LANES), BF16), out((total, features), BF16), out((1, features))],
    )(panels, rel_vecs, edges, pairs, rows, *parts)
    got = lax.all_to_all(send, ("bucket", "entity"), split_axis=0, concat_axis=0, tiled=True)
    [panel_grad] = call(
        panel_kernel, [out((1, features, features))], 2 * total * features * features, 4 * features * features
    )(grad, *parts)
    [ent_grad] = call(lambda *refs: sum_kernel(width, *refs), [out((width, shard_rows))])(got)
    return ent_grad.T, panel_grad, rel_grad


def solution(mesh):
    both = ("bucket", "entity")
    placed = (
        P("entity", None),
        P(both, None, None),
        P(both, None),
        P(both, None, None),
        P(both, None, None),
        P(both, None, None),
        P(both, None, None),
        P(both),
    )
    return jax.shard_map(
        body,
        mesh=mesh,
        in_specs=placed,
        out_specs=(P("entity", "bucket"), P(both, None, None), P(both, None)),
        check_vma=False,
    )
```

time: 143 us -> 31.5 us (0.22)
  waiting for transfers between devices: 74.5 us -> 11.4 us
  other arithmetic: 22.3 us -> 0 us
  between operations: 14.9 us -> 1.36 us
  matrix products: 8.99 us -> 0 us
  local copies, waits for them, and re-layouts: 10.2 us -> 2.6 us
  Pallas kernels: 0 us -> 4.7 us
    unnamed x2 -> x0, waiting for transfers between devices: 67.8 us -> none
    scatter-add x4 -> x0, other arithmetic: 13.1 us -> none  [the longest x1 6.67 us: block_terms(): grad_proj.at[cand_one.reshape(-1)].add(grad_cand.reshape(-1, feature_count))]
    dot_general x6 -> x0, matrix products: 8.99 us -> none  [the longest x1 2.02 us: block_terms(): jnp.einsum('ben,bed->bnd', weight_b, centers, preferred_element_type=jnp....]
    gather x4 -> x0, local copies, waits for them, and re-layouts: 6.97 us -> none  [the longest x1 3.96 us: block_terms(): cand_rows = jnp.take(projected, cand_one, axis=0)]
    ppermute x0 -> x6, starting transfers between devices: none -> 5.25 us  [swap(): return lax.ppermute(x, 'entity', [(i, i ^ s) for i in range(shards)])]
    all_to_all x3 -> x1, starting transfers between devices: 11 us -> 5.94 us  [body(): lax.all_to_all(send, ('bucket', 'entity'), split_axis=0, concat_axis=0, t...]
    pallas_call x0 -> x5, Pallas kernels: none -> 4.7 us  [run(): pl.pallas_call(kernel, out_shape=outs, in_specs=[smem] * len(scalars) + [...]
    ppermute x0 -> x6, waiting for transfers between devices: none -> 4.44 us  [swap(): return lax.ppermute(x, 'entity', [(i, i ^ s) for i in range(shards)])]
  transfers between devices with their start and end apart: 4 -> 7, of which waited for: 3 -> 4; matrix products, arithmetic and copies ran while one was open for 6% -> 0% of each run, Pallas kernels for 0% -> 5%
where the time goes in v1:
time: 31.5 us; the launch traced here: 31.2 us
  waiting for transfers between devices  11.4 us (36%)
  starting transfers between devices  11.2 us (36%)
  Pallas kernels  4.7 us (15%)
  local copies, waits for them, and re-layouts  2.6 us (8%)
  between operations  1.36 us (4%)
    all_to_all x1, waiting for transfers between devices, body(): lax.all_to_all(send, ('bucket', 'entity'), split_axis=0, concat_axis=0, t...  6.94 us
    all_to_all x1, starting transfers between devices, body(): lax.all_to_all(send, ('bucket', 'entity'), split_axis=0, concat_axis=0, t...  5.94 us
    ppermute x6, starting transfers between devices, swap(): return lax.ppermute(x, 'entity', [(i, i ^ s) for i in range(shards)])  5.25 us
    pallas_call x5, Pallas kernels, run(): pl.pallas_call(kernel, out_shape=outs, in_specs=[smem] * len(scalars) + [...  4.7 us
    ppermute x6, waiting for transfers between devices, swap(): return lax.ppermute(x, 'entity', [(i, i ^ s) for i in range(shards)])  4.44 us
    unnamed x16, local copies, waits for them, and re-layouts  2.6 us
  transfers between devices with their start and end apart: 7, of which 4 were waited for; matrix products, arithmetic and copies ran while one was open for 0% of the time, Pallas kernels for 5%

profile of v1, /device:TPU:0, one launch (start us, length us, event | category | flops | bytes accessed | tf_op | source)
XLA Modules:
  0.0 31.2 jit_solution(3530093081522037590)
XLA Ops:
  0.6 3.0 %collective-permute-start.1 = (s32[1,4,16]{2,1,0:T(4,128)}, s32[1,4,16]{2,1,0:T(4,128)S(1)}, u32[]{:S(2)}, u32[]{:S(2)}) collective-permute-start(s32[1,4,16]{2,1,0:T(4,128)} %refs_1_.2), channel_id=1, source_target_pairs={{0,2},{1,3},{2,0},{3,1},{4,6},{5,7},{6,4},{7,5},{8,10},{9,11},{10,... | collective-permute-start | bytes 776 | tf_op jit(solution)/shard_map/ppermute | solution.py:183
  3.7 0.0 collective-permute-start
  3.7 0.2 collective-permute-start.2
  3.9 1.6 %collective-permute-done.1.refs_3_ = s32[1,4,16]{2,1,0:T(4,128)S(1)} collective-permute-done((s32[1,4,16]{2,1,0:T(4,128)}, s32[1,4,16]{2,1,0:T(4,128)S(1)}, u32[]{:S(2)}, u32[]{:S(2)}) %collective-permute-start.1) | collective-permute-done | bytes 288 | tf_op jit(solution)/shard_map/ppermute | solution.py:183
  5.4 0.0 collective-permute-done.refs_2_
  5.4 1.4 %collective-permute-done.2.refs_4_ = s32[1,4,16]{2,1,0:T(4,128)S(1)} collective-permute-done((s32[1,4,16]{2,1,0:T(4,128)}, s32[1,4,16]{2,1,0:T(4,128)S(1)}, u32[]{:S(2)}, u32[]{:S(2)}) %collective-permute-start.2) | collective-permute-done | bytes 288 | tf_op jit(solution)/shard_map/ppermute | solution.py:183
  6.9 0.0 copy-start
  6.9 1.2 %copy-done = bf16[1024,512]{1,0:T(8,128)(2,1)S(1)} copy-done((bf16[1024,512]{1,0:T(8,128)(2,1)S(1)}, bf16[1024,512]{1,0:T(8,128)(2,1)}, u32[]{:S(2)}) %copy-start) | copy-done | bytes 1048600
  8.1 0.0 copy-start.2
  8.1 0.7 %copy-done.2 = s32[1,4,16]{2,1,0:T(4,128)S(1)} copy-done((s32[1,4,16]{2,1,0:T(4,128)S(1)}, s32[1,4,16]{2,1,0:T(4,128)}, u32[]{:S(2)}) %copy-start.2) | copy-done | bytes 280
  8.8 0.0 copy-start.7
  8.8 0.0 copy-start.1
  8.8 0.4 %shard_map.104 = (bf16[16,512]{1,0:T(8,128)(2,1)S(1)}, bf16[16,512]{1,0:T(8,128)(2,1)S(1)}, bf16[16,512]{1,0:T(8,128)(2,1)S(1)}, bf16[16,512]{1,0:T(8,128)(2,1)S(1)}) custom-call(bf16[1024,512]{1,0:T(8,128)(2,1)S(1)} %copy-done, s32[1,4,16]{2,1,0:T(4,128)S(1)} %copy-done.2, s32[1,4,16]{2,1,0:T(4,128)S(1)} %collective-permute-done.refs_2_, ...), custom_call_target="tpu_custom_call" | custom-call | tf_op jit(solution)/shard_map/pallas_call | solution.py:47
  9.2 0.0 copy-start.4
  9.2 0.6 %collective-permute-start.3 = (bf16[16,512]{1,0:T(8,128)(2,1)S(1)}, bf16[16,512]{1,0:T(8,128)(2,1)S(1)}, u32[]{:S(2)}, u32[]{:S(2)}) collective-permute-start(bf16[16,512]{1,0:T(8,128)(2,1)S(1)} %get-tuple-element.17), channel_id=1, source_target_pairs={{0,1},{1,0},{2,3},{3,2},{4,5},{5,4},{6,7},{7,6},{8,9},{9,8},{10,11... | collective-permute-start | bytes 49160 | tf_op jit(solution)/shard_map/ppermute | solution.py:183
  9.7 0.2 collective-permute-start.4
  9.9 1.3 %collective-permute-start.5 = (bf16[16,512]{1,0:T(8,128)(2,1)S(1)}, bf16[16,512]{1,0:T(8,128)(2,1)S(1)}, u32[]{:S(2)}, u32[]{:S(2)}) collective-permute-start(bf16[16,512]{1,0:T(8,128)(2,1)S(1)} %get-tuple-element.19), channel_id=1, source_target_pairs={{0,3},{1,2},{2,1},{3,0},{4,7},{5,6},{6,5},{7,4},{8,11},{9,10},{10,... | collective-permute-start | bytes 49160 | tf_op jit(solution)/shard_map/ppermute | solution.py:183
  11.8 0.0 copy-done.7
  11.9 0.0 copy-done.4
  11.9 0.0 copy-done.3
  11.9 0.0 copy-done.6
  11.9 0.2 shard_map.103
  12.1 0.0 collective-permute-done.3.refs_6_.refs_1_
  12.1 1.4 %collective-permute-done.4.refs_7_.refs_2_ = bf16[16,512]{1,0:T(8,128)(2,1)S(1)} collective-permute-done((bf16[16,512]{1,0:T(8,128)(2,1)S(1)}, bf16[16,512]{1,0:T(8,128)(2,1)S(1)}, u32[]{:S(2)}, u32[]{:S(2)}) %collective-permute-start.4) | collective-permute-done | bytes 16416 | tf_op jit(solution)/shard_map/ppermute | solution.py:183
  13.5 0.0 collective-permute-done.5.refs_8_.refs_3_
  13.5 0.0 copy-done.1
  13.5 0.7 %copy-done.5 = bf16[1,512]{1,0:T(2,128)(2,1)S(1)} copy-done((bf16[1,512]{1,0:T(2,128)(2,1)S(1)}, bf16[1,512]{1,0:T(2,128)(2,1)}, u32[]{:S(2)}) %copy-start.5) | copy-done | bytes 1048
  14.2 1.6 %shard_map.105 = (bf16[32,16,128]{2,1,0:T(8,128)(2,1)}, bf16[64,512]{1,0:T(8,128)(2,1)S(1)}, f32[1,512]{1,0:T(1,128)}) custom-call(bf16[1,512,512]{2,1,0:T(8,128)(2,1)S(1)} %copy-done.1, bf16[1,512]{1,0:T(2,128)(2,1)S(1)} %copy-done.5, f32[64,64]{1,0:T(8,128)S(1)} %get-tuple-element.13.refs_2_, f32[64,64]{1,0:T(8,128)S(1)} %get-tuple-element.14.refs_3_, ...), custom_call_target="tpu_custom_call" | custom-call | tf_op jit(solution)/shard_map/pallas_call | solution.py:47
  15.8 5.9 %all-to-all-start = ((bf16[32,16,128]{2,1,0:T(8,128)(2,1)}), bf16[32,16,128]{2,1,0:T(8,128)(2,1)S(1)}, u32[]{:S(2)}, u32[]{:S(2)}) async-start(bf16[32,16,128]{2,1,0:T(8,128)(2,1)} %get-tuple-element.20), calls=%async_computation | async-start | bytes 262144 | tf_op jit(solution)/shard_map/all_to_all | solution.py:198
  21.7 1.3 %shard_map.107 = f32[1,512,512]{2,1,0:T(8,128)} custom-call(bf16[64,512]{1,0:T(8,128)(2,1)S(1)} %get-tuple-element.21.grad_ref, bf16[16,512]{1,0:T(8,128)(2,1)S(1)} %get-tuple-element.16.refs_5_.refs_0_, bf16[16,512]{1,0:T(8,128)(2,1)S(1)} %collective-permute-done.3.refs_6_.refs_1_, bf16[16,512]{1,0:T(8,128)(2,1)S(1)} %collective-permute-done.4.refs_7_.refs_2_, ...), custom_call_target="tpu_custom_call" | custom-call | flops 33554432 | bytes 1048576 | tf_op jit(solution)/shard_map/pallas_call | solution.py:47
  23.0 6.9 %all-to-all-done.refs_0_ = bf16[32,16,128]{2,1,0:T(8,128)(2,1)S(1)} async-done(((bf16[32,16,128]{2,1,0:T(8,128)(2,1)}), bf16[32,16,128]{2,1,0:T(8,128)(2,1)S(1)}, u32[]{:S(2)}, u32[]{:S(2)}) %all-to-all-start) | async-done | bytes 131104 | tf_op jit(solution)/shard_map/all_to_all | solution.py:198
  29.9 1.3 %shard_map.106 = f32[64,1024]{1,0:T(8,128)} custom-call(bf16[32,16,128]{2,1,0:T(8,128)(2,1)S(1)} %all-to-all-done.refs_0_), custom_call_target="tpu_custom_call" | custom-call | tf_op jit(solution)/shard_map/pallas_call | solution.py:47
  (3 shorter events, 0.0 us)
Async XLA Ops:
  0.6 4.8 %collective-permute-start.1 = (s32[1,4,16]{2,1,0:T(4,128)}, s32[1,4,16]{2,1,0:T(4,128)S(1)}, u32[]{:S(2)}, u32[]{:S(2)}) collective-permute-start(s32[1,4,16]{2,1,0:T(4,128)} %refs_1_.2), channel_id=1, source_target_pairs={{0,2},{1,3},{2,0},{3,1},{4,6},{5,7},{6,4},{7,5},{8,10},{9,11},{10,... | collective-permute-start | bytes 776 | tf_op jit(solution)/shard_map/ppermute | solution.py:183
  3.7 1.8 %collective-permute-start = (s32[1,4,16]{2,1,0:T(4,128)}, s32[1,4,16]{2,1,0:T(4,128)S(1)}, u32[]{:S(2)}, u32[]{:S(2)}) collective-permute-start(s32[1,4,16]{2,1,0:T(4,128)} %refs_1_.2), channel_id=1, source_target_pairs={{0,1},{1,0},{2,3},{3,2},{4,5},{5,4},{6,7},{7,6},{8,9},{9,8},{10,11... | collective-permute-start | bytes 776 | tf_op jit(solution)/shard_map/ppermute | solution.py:183
  3.7 3.2 %collective-permute-start.2 = (s32[1,4,16]{2,1,0:T(4,128)}, s32[1,4,16]{2,1,0:T(4,128)S(1)}, u32[]{:S(2)}, u32[]{:S(2)}) collective-permute-start(s32[1,4,16]{2,1,0:T(4,128)} %refs_1_.2), channel_id=1, source_target_pairs={{0,3},{1,2},{2,1},{3,0},{4,7},{5,6},{6,5},{7,4},{8,11},{9,10},{10,... | collective-permute-start | bytes 776 | tf_op jit(solution)/shard_map/ppermute | solution.py:183
  6.9 1.2 %copy-start = (bf16[1024,512]{1,0:T(8,128)(2,1)S(1)}, bf16[1024,512]{1,0:T(8,128)(2,1)}, u32[]{:S(2)}) copy-start(bf16[1024,512]{1,0:T(8,128)(2,1)} %refs_0_.2) | copy-start | bytes 3145732
  8.1 0.7 %copy-start.2 = (s32[1,4,16]{2,1,0:T(4,128)S(1)}, s32[1,4,16]{2,1,0:T(4,128)}, u32[]{:S(2)}) copy-start(s32[1,4,16]{2,1,0:T(4,128)} %refs_1_.2) | copy-start | bytes 772
  8.8 3.0 %copy-start.7 = (s32[1,2,128]{2,1,0:T(2,128)S(1)}, s32[1,2,128]{2,1,0:T(2,128)}, u32[]{:S(2)}) copy-start(s32[1,2,128]{2,1,0:T(2,128)} %tail_ref.1) | copy-start | bytes 3076
  8.8 4.7 %copy-start.1 = (bf16[1,512,512]{2,1,0:T(8,128)(2,1)S(1)}, bf16[1,512,512]{2,1,0:T(8,128)(2,1)}, u32[]{:S(2)}) copy-start(bf16[1,512,512]{2,1,0:T(8,128)(2,1)} %refs_0_.3) | copy-start | bytes 1572868
  9.2 2.7 %copy-start.4 = (s32[1,2,512]{2,1,0:T(2,128)S(1)}, s32[1,2,512]{2,1,0:T(2,128)}, u32[]{:S(2)}) copy-start(s32[1,2,512]{2,1,0:T(2,128)} %neg_ref.1) | copy-start | bytes 12292
  9.2 2.9 %collective-permute-start.3 = (bf16[16,512]{1,0:T(8,128)(2,1)S(1)}, bf16[16,512]{1,0:T(8,128)(2,1)S(1)}, u32[]{:S(2)}, u32[]{:S(2)}) collective-permute-start(bf16[16,512]{1,0:T(8,128)(2,1)S(1)} %get-tuple-element.17), channel_id=1, source_target_pairs={{0,1},{1,0},{2,3},{3,2},{4,5},{5,4},{6,7},{7,6},{8,9},{9,8},{10,11... | collective-permute-start | bytes 49160 | tf_op jit(solution)/shard_map/ppermute | solution.py:183
  9.7 2.1 %copy-start.3 = (s32[1,4,16]{2,1,0:T(4,128)S(1)}, s32[1,4,16]{2,1,0:T(4,128)}, u32[]{:S(2)}) copy-start(s32[1,4,16]{2,1,0:T(4,128)} %refs_1_.2) | copy-start | bytes 772
  9.7 3.7 %collective-permute-start.4 = (bf16[16,512]{1,0:T(8,128)(2,1)S(1)}, bf16[16,512]{1,0:T(8,128)(2,1)S(1)}, u32[]{:S(2)}, u32[]{:S(2)}) collective-permute-start(bf16[16,512]{1,0:T(8,128)(2,1)S(1)} %get-tuple-element.18), channel_id=1, source_target_pairs={{0,2},{1,3},{2,0},{3,1},{4,6},{5,7},{6,4},{7,5},{8,10},{9,11},{10,... | collective-permute-start | bytes 49160 | tf_op jit(solution)/shard_map/ppermute | solution.py:183
  9.9 1.9 %copy-start.6 = (s32[1,2,128]{2,1,0:T(2,128)S(1)}, s32[1,2,128]{2,1,0:T(2,128)}, u32[]{:S(2)}) copy-start(s32[1,2,128]{2,1,0:T(2,128)} %head_ref.1) | copy-start | bytes 3076
  9.9 3.6 %collective-permute-start.5 = (bf16[16,512]{1,0:T(8,128)(2,1)S(1)}, bf16[16,512]{1,0:T(8,128)(2,1)S(1)}, u32[]{:S(2)}, u32[]{:S(2)}) collective-permute-start(bf16[16,512]{1,0:T(8,128)(2,1)S(1)} %get-tuple-element.19), channel_id=1, source_target_pairs={{0,3},{1,2},{2,1},{3,0},{4,7},{5,6},{6,5},{7,4},{8,11},{9,10},{10,... | collective-permute-start | bytes 49160 | tf_op jit(solution)/shard_map/ppermute | solution.py:183
  13.5 0.7 %copy-start.5 = (bf16[1,512]{1,0:T(2,128)(2,1)S(1)}, bf16[1,512]{1,0:T(2,128)(2,1)}, u32[]{:S(2)}) copy-start(bf16[1,512]{1,0:T(2,128)(2,1)} %refs_1_.3) | copy-start | bytes 3076
  15.8 14.2 %all-to-all-start = ((bf16[32,16,128]{2,1,0:T(8,128)(2,1)}), bf16[32,16,128]{2,1,0:T(8,128)(2,1)S(1)}, u32[]{:S(2)}, u32[]{:S(2)}) async-start(bf16[32,16,128]{2,1,0:T(8,128)(2,1)} %get-tuple-element.20), calls=%async_computation | async-start | bytes 262144 | tf_op jit(solution)/shard_map/all_to_all | solution.py:198

commit v2 on v1

--- a/solution.py
+++ b/solution.py
@@ -39,24 +39,41 @@
     return jnp.sum(jnp.where(iota((n, n), 0) == iota((n, n), 1), row, 0.0), axis=1, keepdims=True)
 
 
-def call(kernel, outs, flops=0, nbytes=0):
-    vmem = pl.BlockSpec(memory_space=pltpu.VMEM)
-    smem = pl.BlockSpec(memory_space=pltpu.SMEM)
-
-    def run(*args, scalars=()):
-        return pl.pallas_call(
-            kernel,
-            out_shape=outs,
-            in_specs=[smem] * len(scalars) + [vmem] * len(args),
-            out_specs=[vmem] * len(outs),
-            compiler_params=pltpu.CompilerParams(vmem_limit_bytes=VMEM_BYTES),
-            cost_estimate=pl.CostEstimate(flops=flops, bytes_accessed=nbytes, transcendentals=0),
-        )(*scalars, *args)
-
-    return run
-
-
-def counts_kernel(count_ref, head_ref, tail_ref, neg_ref, req_ref, edges_ref, pairs_ref, rows_ref):
+def call(kernel, ins, outs, scratch=(), flops=0, nbytes=0):
+    return pl.pallas_call(
+        kernel,
+        out_shape=outs,
+        in_specs=[pl.BlockSpec(memory_space=space) for space in ins],
+        out_specs=[pl.BlockSpec(memory_space=pltpu.VMEM)] * len(outs),
+        scratch_shapes=list(scratch),
+        compiler_params=pltpu.CompilerParams(vmem_limit_bytes=VMEM_BYTES),
+        cost_estimate=pl.CostEstimate(flops=flops, bytes_accessed=nbytes, transcendentals=0),
+    )
+
+
+def prepare_kernel(
+    count_ref, head_hbm, tail_hbm, neg_hbm, req_hbm, table_hbm, panel_hbm, rel_hbm,
+    edges_ref, pairs_ref, rows_ref, req_ref, table_ref, panel_ref, rel_ref,
+    head_ref, tail_ref, neg_ref, sems,
+):
+    moves = [
+        pltpu.make_async_copy(src, dst, sems.at[i])
+        for i, (src, dst) in enumerate(
+            [
+                (head_hbm, head_ref),
+                (tail_hbm, tail_ref),
+                (neg_hbm, neg_ref),
+                (req_hbm, req_ref),
+                (rel_hbm, rel_ref),
+                (table_hbm, table_ref),
+                (panel_hbm, panel_ref),
+            ]
+        )
+    ]
+    for move in moves:
+        move.start()
+    for move in moves[:4]:
+        move.wait()
     shards, cap = req_ref.shape[1:]
     total = shards * cap
     me = lax.axis_index("entity")
@@ -82,6 +99,8 @@
     high = jnp.floor(column * (1.0 / DIGIT))
     low = column - high * DIGIT
     rows_ref[...] = jnp.where(iota((total, LANES), 1) < 96, high, low)
+    for move in moves[4:]:
+        move.wait()
 
 
 def pick_kernel(*refs):
@@ -185,21 +204,45 @@
     def out(shape, dtype=F32):
         return jax.ShapeDtypeStruct(shape, dtype)
 
-    asked = [requests] + [swap(requests, s) for s in range(1, shards)]
-    edges, pairs, rows = call(
-        counts_kernel, [out((total, total)), out((total, total)), out((total, LANES))]
-    )(head_slots, tail_slots, negatives, requests, scalars=(block_count,))
-    found = call(pick_kernel, [out((cap, features), BF16)] * shards)(ent_table, *asked)
+    def like(x):
+        return out(x.shape, x.dtype)
+
+    vmem, hbm = pltpu.VMEM, pltpu.HBM
+    asked = [swap(requests, s) for s in range(1, shards)]
+    edges, pairs, rows, own, table, panel, rel = call(
+        prepare_kernel,
+        [pltpu.SMEM] + [hbm] * 7,
+        [out((total, total)), out((total, total)), out((total, LANES))]
+        + [like(x) for x in (requests, ent_table, panels, rel_vecs)],
+        [
+            pltpu.VMEM(head_slots.shape, I32),
+            pltpu.VMEM(tail_slots.shape, I32),
+            pltpu.VMEM(negatives.shape, I32),
+            pltpu.SemaphoreType.DMA((7,)),
+        ],
+    )(
+        block_count,
+        *[
+            pltpu.with_memory_space_constraint(x, hbm)
+            for x in (head_slots, tail_slots, negatives, requests, ent_table, panels, rel_vecs)
+        ]
+    )
+    found = call(pick_kernel, [vmem] * (1 + shards), [out((cap, features), BF16)] * shards)(table, own, *asked)
     parts = [found[0]] + [swap(found[s], s) for s in range(1, shards)]
     send, grad, rel_grad = call(
         lambda *refs: terms_kernel(buckets, negatives.shape[2], *refs),
+        [vmem] * (5 + shards),
         [out((buckets * shards, cap, LANES), BF16), out((total, features), BF16), out((1, features))],
-    )(panels, rel_vecs, edges, pairs, rows, *parts)
+    )(panel, rel, edges, pairs, rows, *parts)
     got = lax.all_to_all(send, ("bucket", "entity"), split_axis=0, concat_axis=0, tiled=True)
     [panel_grad] = call(
-        panel_kernel, [out((1, features, features))], 2 * total * features * features, 4 * features * features
+        panel_kernel,
+        [vmem] * (1 + shards),
+        [out((1, features, features))],
+        flops=2 * total * features * features,
+        nbytes=4 * features * features,
     )(grad, *parts)
-    [ent_grad] = call(lambda *refs: sum_kernel(width, *refs), [out((width, shard_rows))])(got)
+    [ent_grad] = call(lambda *refs: sum_kernel(width, *refs), [vmem], [out((width, shard_rows))])(got)
     return ent_grad.T, panel_grad, rel_grad
 
 

time: 31.5 us -> 29 us (0.921)
  local copies, waits for them, and re-layouts: 2.6 us -> 0 us
  Pallas kernels: 4.7 us -> 6.03 us
  waiting for transfers between devices: 11.4 us -> 10.5 us
    unnamed x16 -> x0, local copies, waits for them, and re-layouts: 2.6 us -> none
    pallas_call x5, Pallas kernels: 4.7 us -> 6.03 us  [the longest x1 1.58 us: body(): call(lambda *refs: terms_kernel(buckets, negatives.shape[2], *refs), [vme...]
    ppermute x6, waiting for transfers between devices: 4.44 us -> 3.55 us  [swap(): return lax.ppermute(x, 'entity', [(i, i ^ s) for i in range(shards)])]
  transfers between devices with their start and end apart: 7 -> 7, of which waited for: 4 -> 3; matrix products, arithmetic and copies ran while one was open for 0% -> 0% of each run, Pallas kernels for 5% -> 10%
where the time goes in v2:
time: 29 us; the launch traced here: 28.7 us
  starting transfers between devices  10.9 us (38%)
  waiting for transfers between devices  10.5 us (36%)
  Pallas kernels  6.03 us (21%)
  between operations  1.34 us (5%)
    all_to_all x1, waiting for transfers between devices, body(): lax.all_to_all(send, ('bucket', 'entity'), split_axis=0, concat_axis=0, t...  6.94 us
    all_to_all x1, starting transfers between devices, body(): lax.all_to_all(send, ('bucket', 'entity'), split_axis=0, concat_axis=0, t...  5.75 us
    ppermute x6, starting transfers between devices, swap(): return lax.ppermute(x, 'entity', [(i, i ^ s) for i in range(shards)])  5.13 us
    ppermute x6, waiting for transfers between devices, swap(): return lax.ppermute(x, 'entity', [(i, i ^ s) for i in range(shards)])  3.55 us
    pallas_call x1, Pallas kernels, body(): call(lambda *refs: terms_kernel(buckets, negatives.shape[2], *refs), [vme...  1.58 us
    pallas_call x1, Pallas kernels, body(): call(prepare_kernel, [pltpu.SMEM] + [hbm] * 7, [out((total, total)), out(...  1.5 us
    pallas_call x1, Pallas kernels, body(): call(lambda *refs: sum_kernel(width, *refs), [vmem], [out((width, shard_r...  1.31 us
    pallas_call x1, Pallas kernels, body(): call(panel_kernel, [vmem] * (1 + shards), [out((1, features, features))],...  1.29 us
  transfers between devices with their start and end apart: 7, of which 3 were waited for; matrix products, arithmetic and copies ran while one was open for 0% of the time, Pallas kernels for 10%

profile of v2, /device:TPU:0, one launch (start us, length us, event | category | flops | bytes accessed | tf_op | source)
XLA Modules:
  0.0 28.7 jit_solution(16991072380862406702)
XLA Ops:
  0.6 0.5 %collective-permute-start = (s32[1,4,16]{2,1,0:T(4,128)}, s32[1,4,16]{2,1,0:T(4,128)S(1)}, u32[]{:S(2)}, u32[]{:S(2)}) collective-permute-start(s32[1,4,16]{2,1,0:T(4,128)} %req_hbm.1), channel_id=1, source_target_pairs={{0,1},{1,0},{2,3},{3,2},{4,5},{5,4},{6,7},{7,6},{8,9},{9,8},{10,11... | collective-permute-start | bytes 776 | tf_op jit(solution)/shard_map/ppermute | solution.py:202
  1.2 2.6 %collective-permute-start.2 = (s32[1,4,16]{2,1,0:T(4,128)}, s32[1,4,16]{2,1,0:T(4,128)S(1)}, u32[]{:S(2)}, u32[]{:S(2)}) collective-permute-start(s32[1,4,16]{2,1,0:T(4,128)} %req_hbm.1), channel_id=1, source_target_pairs={{0,3},{1,2},{2,1},{3,0},{4,7},{5,6},{6,5},{7,4},{8,11},{9,10},{10,... | collective-permute-start | bytes 776 | tf_op jit(solution)/shard_map/ppermute | solution.py:202
  3.8 0.0 collective-permute-start.1
  4.5 1.5 %shard_map.103 = (f32[64,64]{1,0:T(8,128)S(1)}, f32[64,64]{1,0:T(8,128)S(1)}, f32[64,128]{1,0:T(8,128)S(1)}, s32[1,4,16]{2,1,0:T(4,128)S(1)}, bf16[1024,512]{1,0...) custom-call(s32[1]{0:T(128)S(6)} %copy.11.count_ref, s32[1,2,128]{2,1,0:T(2,128)} %head_hbm.1, ...), custom_call_target="tpu_custom_call" | custom-call | tf_op jit(solution)/shard_map/pallas_call | solution.py:212
  6.0 0.0 collective-permute-done.refs_2_
  6.0 0.0 collective-permute-done.2.refs_4_
  6.0 1.6 %collective-permute-done.1.refs_3_ = s32[1,4,16]{2,1,0:T(4,128)S(1)} collective-permute-done((s32[1,4,16]{2,1,0:T(4,128)}, s32[1,4,16]{2,1,0:T(4,128)S(1)}, u32[]{:S(2)}, u32[]{:S(2)}) %collective-permute-start.1) | collective-permute-done | bytes 288 | tf_op jit(solution)/shard_map/ppermute | solution.py:202
  7.6 0.4 %shard_map.104 = (bf16[16,512]{1,0:T(8,128)(2,1)S(1)}, bf16[16,512]{1,0:T(8,128)(2,1)S(1)}, bf16[16,512]{1,0:T(8,128)(2,1)S(1)}, bf16[16,512]{1,0:T(8,128)(2,1)S(1)}) custom-call(bf16[1024,512]{1,0:T(8,128)(2,1)S(1)} %get-tuple-element.22.refs_0_, s32[1,4,16]{2,1,0:T(4,128)S(1)} %get-tuple-element.23.refs_1_, s32[1,4,16]{2,1,0:T(4,128)S(1)} %collective-permute-done.refs_2_, ...), custom_call_target="tpu_custom_call" | custom-call | tf_op jit(solution)/shard_map/pallas_call | solution.py:230
  8.0 0.1 collective-permute-start.3
  8.0 0.5 %collective-permute-start.4 = (bf16[16,512]{1,0:T(8,128)(2,1)S(1)}, bf16[16,512]{1,0:T(8,128)(2,1)S(1)}, u32[]{:S(2)}, u32[]{:S(2)}) collective-permute-start(bf16[16,512]{1,0:T(8,128)(2,1)S(1)} %get-tuple-element.26), channel_id=1, source_target_pairs={{0,2},{1,3},{2,0},{3,1},{4,6},{5,7},{6,4},{7,5},{8,10},{9,11},{10,... | collective-permute-start | bytes 49160 | tf_op jit(solution)/shard_map/ppermute | solution.py:202
  8.5 1.4 %collective-permute-start.5 = (bf16[16,512]{1,0:T(8,128)(2,1)S(1)}, bf16[16,512]{1,0:T(8,128)(2,1)S(1)}, u32[]{:S(2)}, u32[]{:S(2)}) collective-permute-start(bf16[16,512]{1,0:T(8,128)(2,1)S(1)} %get-tuple-element.27), channel_id=1, source_target_pairs={{0,3},{1,2},{2,1},{3,0},{4,7},{5,6},{6,5},{7,4},{8,11},{9,10},{10,... | collective-permute-start | bytes 49160 | tf_op jit(solution)/shard_map/ppermute | solution.py:202
  9.9 0.0 collective-permute-done.3.refs_6_.refs_1_
  9.9 2.0 %collective-permute-done.4.refs_7_.refs_2_ = bf16[16,512]{1,0:T(8,128)(2,1)S(1)} collective-permute-done((bf16[16,512]{1,0:T(8,128)(2,1)S(1)}, bf16[16,512]{1,0:T(8,128)(2,1)S(1)}, u32[]{:S(2)}, u32[]{:S(2)}) %collective-permute-start.4) | collective-permute-done | bytes 16416 | tf_op jit(solution)/shard_map/ppermute | solution.py:202
  11.9 0.0 collective-permute-done.5.refs_8_.refs_3_
  11.9 1.6 %shard_map.105 = (bf16[32,16,128]{2,1,0:T(8,128)(2,1)}, bf16[64,512]{1,0:T(8,128)(2,1)S(1)}, f32[1,512]{1,0:T(1,128)}) custom-call(bf16[1,512,512]{2,1,0:T(8,128)(2,1)S(1)} %get-tuple-element.17.refs_0_, bf16[1,512]{1,0:T(2,128)(2,1)S(1)} %get-tuple-element.18.refs_1_, f32[64,64]{1,0:T(8,128)S(1)} %get-tuple-element.19.refs_2_, ...), custom_call_target="tpu_custom_call" | custom-call | tf_op jit(solution)/shard_map/pallas_call | solution.py:232
  13.4 5.8 %all-to-all-start = ((bf16[32,16,128]{2,1,0:T(8,128)(2,1)}), bf16[32,16,128]{2,1,0:T(8,128)(2,1)S(1)}, u32[]{:S(2)}, u32[]{:S(2)}) async-start(bf16[32,16,128]{2,1,0:T(8,128)(2,1)} %get-tuple-element.28), calls=%async_computation | async-start | bytes 262144 | tf_op jit(solution)/shard_map/all_to_all | solution.py:237
  19.2 1.3 %shard_map.107 = f32[1,512,512]{2,1,0:T(8,128)} custom-call(bf16[64,512]{1,0:T(8,128)(2,1)S(1)} %get-tuple-element.29.grad_ref, bf16[16,512]{1,0:T(8,128)(2,1)S(1)} %get-tuple-element.24.refs_5_.refs_0_, bf16[16,512]{1,0:T(8,128)(2,1)S(1)} %collective-permute-done.3.refs_6_.refs_1_, bf16[16,512]{1,0:T(8,128)(2,1)S(1)} %collective-permute-done.4.refs_7_.refs_2_, ...), custom_call_target="tpu_custom_call" | custom-call | flops 33554432 | bytes 1048576 | tf_op jit(solution)/shard_map/pallas_call | solution.py:238
  20.5 6.9 %all-to-all-done.refs_0_ = bf16[32,16,128]{2,1,0:T(8,128)(2,1)S(1)} async-done(((bf16[32,16,128]{2,1,0:T(8,128)(2,1)}), bf16[32,16,128]{2,1,0:T(8,128)(2,1)S(1)}, u32[]{:S(2)}, u32[]{:S(2)}) %all-to-all-start) | async-done | bytes 131104 | tf_op jit(solution)/shard_map/all_to_all | solution.py:237
  27.4 1.3 %shard_map.106 = f32[64,1024]{1,0:T(8,128)} custom-call(bf16[32,16,128]{2,1,0:T(8,128)(2,1)S(1)} %all-to-all-done.refs_0_), custom_call_target="tpu_custom_call" | custom-call | tf_op jit(solution)/shard_map/pallas_call | solution.py:245
Async XLA Ops:
  0.6 5.4 %collective-permute-start = (s32[1,4,16]{2,1,0:T(4,128)}, s32[1,4,16]{2,1,0:T(4,128)S(1)}, u32[]{:S(2)}, u32[]{:S(2)}) collective-permute-start(s32[1,4,16]{2,1,0:T(4,128)} %req_hbm.1), channel_id=1, source_target_pairs={{0,1},{1,0},{2,3},{3,2},{4,5},{5,4},{6,7},{7,6},{8,9},{9,8},{10,11... | collective-permute-start | bytes 776 | tf_op jit(solution)/shard_map/ppermute | solution.py:202
  1.2 4.9 %collective-permute-start.2 = (s32[1,4,16]{2,1,0:T(4,128)}, s32[1,4,16]{2,1,0:T(4,128)S(1)}, u32[]{:S(2)}, u32[]{:S(2)}) collective-permute-start(s32[1,4,16]{2,1,0:T(4,128)} %req_hbm.1), channel_id=1, source_target_pairs={{0,3},{1,2},{2,1},{3,0},{4,7},{5,6},{6,5},{7,4},{8,11},{9,10},{10,... | collective-permute-start | bytes 776 | tf_op jit(solution)/shard_map/ppermute | solution.py:202
  3.8 3.8 %collective-permute-start.1 = (s32[1,4,16]{2,1,0:T(4,128)}, s32[1,4,16]{2,1,0:T(4,128)S(1)}, u32[]{:S(2)}, u32[]{:S(2)}) collective-permute-start(s32[1,4,16]{2,1,0:T(4,128)} %req_hbm.1), channel_id=1, source_target_pairs={{0,2},{1,3},{2,0},{3,1},{4,6},{5,7},{6,4},{7,5},{8,10},{9,11},{10,... | collective-permute-start | bytes 776 | tf_op jit(solution)/shard_map/ppermute | solution.py:202
  8.0 1.9 %collective-permute-start.3 = (bf16[16,512]{1,0:T(8,128)(2,1)S(1)}, bf16[16,512]{1,0:T(8,128)(2,1)S(1)}, u32[]{:S(2)}, u32[]{:S(2)}) collective-permute-start(bf16[16,512]{1,0:T(8,128)(2,1)S(1)} %get-tuple-element.25), channel_id=1, source_target_pairs={{0,1},{1,0},{2,3},{3,2},{4,5},{5,4},{6,7},{7,6},{8,9},{9,8},{10,11... | collective-permute-start | bytes 49160 | tf_op jit(solution)/shard_map/ppermute | solution.py:202
  8.0 3.8 %collective-permute-start.4 = (bf16[16,512]{1,0:T(8,128)(2,1)S(1)}, bf16[16,512]{1,0:T(8,128)(2,1)S(1)}, u32[]{:S(2)}, u32[]{:S(2)}) collective-permute-start(bf16[16,512]{1,0:T(8,128)(2,1)S(1)} %get-tuple-element.26), channel_id=1, source_target_pairs={{0,2},{1,3},{2,0},{3,1},{4,6},{5,7},{6,4},{7,5},{8,10},{9,11},{10,... | collective-permute-start | bytes 49160 | tf_op jit(solution)/shard_map/ppermute | solution.py:202
  8.5 3.3 %collective-permute-start.5 = (bf16[16,512]{1,0:T(8,128)(2,1)S(1)}, bf16[16,512]{1,0:T(8,128)(2,1)S(1)}, u32[]{:S(2)}, u32[]{:S(2)}) collective-permute-start(bf16[16,512]{1,0:T(8,128)(2,1)S(1)} %get-tuple-element.27), channel_id=1, source_target_pairs={{0,3},{1,2},{2,1},{3,0},{4,7},{5,6},{6,5},{7,4},{8,11},{9,10},{10,... | collective-permute-start | bytes 49160 | tf_op jit(solution)/shard_map/ppermute | solution.py:202
  13.4 14.0 %all-to-all-start = ((bf16[32,16,128]{2,1,0:T(8,128)(2,1)}), bf16[32,16,128]{2,1,0:T(8,128)(2,1)S(1)}, u32[]{:S(2)}, u32[]{:S(2)}) async-start(bf16[32,16,128]{2,1,0:T(8,128)(2,1)} %get-tuple-element.28), calls=%async_computation | async-start | bytes 262144 | tf_op jit(solution)/shard_map/all_to_all | solution.py:237

commit v3 on v2

--- a/solution.py
+++ b/solution.py
@@ -1,3 +1,5 @@
+import functools
+
 import jax
 import jax.numpy as jnp
 from jax import lax
@@ -39,15 +41,14 @@
     return jnp.sum(jnp.where(iota((n, n), 0) == iota((n, n), 1), row, 0.0), axis=1, keepdims=True)
 
 
-def call(kernel, ins, outs, scratch=(), flops=0, nbytes=0):
+def call(kernel, ins, outs, scratch=(), space=pltpu.VMEM):
     return pl.pallas_call(
         kernel,
         out_shape=outs,
-        in_specs=[pl.BlockSpec(memory_space=space) for space in ins],
-        out_specs=[pl.BlockSpec(memory_space=pltpu.VMEM)] * len(outs),
+        in_specs=[pl.BlockSpec(memory_space=place) for place in ins],
+        out_specs=[pl.BlockSpec(memory_space=space)] * len(outs),
         scratch_shapes=list(scratch),
         compiler_params=pltpu.CompilerParams(vmem_limit_bytes=VMEM_BYTES),
-        cost_estimate=pl.CostEstimate(flops=flops, bytes_accessed=nbytes, transcendentals=0),
     )
 
 
@@ -103,23 +104,20 @@
         move.wait()
 
 
-def pick_kernel(*refs):
-    table_ref, asked, outs = refs[0], refs[1 : 1 + (len(refs) - 1) // 2], refs[1 + (len(refs) - 1) // 2 :]
+def pick_kernel(first, near_ref, other_ref, asked_ref, out_ref):
     me = lax.axis_index("entity")
-    cap = asked[0].shape[2]
-    column = to_column([r[0, pl.ds(me, 1), :] for r in asked]).astype(I32)
-    rows = table_ref.shape[0]
-    hot = (column == iota((column.shape[0], rows), 1)).astype(F32).astype(BF16)
-    found = dot(hot, table_ref[...], (1, 0)).astype(BF16)
-    for s, out in enumerate(outs):
-        out[...] = found[s * cap : (s + 1) * cap]
+    cap = asked_ref.shape[2]
+    for k, table_ref in enumerate((near_ref, other_ref)):
+        column = to_column([asked_ref[0, pl.ds(jnp.bitwise_xor(me, k), 1), :]]).astype(I32)
+        hot = (column == iota((cap, table_ref.shape[0]), 1)).astype(F32).astype(BF16)
+        at = (first ^ k) * cap
+        out_ref[at : at + cap] = dot(hot, table_ref[...], (1, 0)).astype(BF16)
 
 
 def terms_kernel(buckets, negs, *refs):
     panel_ref, rel_ref, edges_ref, pairs_ref, rows_ref = refs[:5]
     send_ref, grad_ref, rel_grad_ref = refs[-3:]
     parts = refs[5:-3]
-    shards = len(parts)
     fetched = jnp.concatenate([r[...] for r in parts], axis=0)
     panel = panel_ref[0]
     proj = dot(fetched, panel, (1, 1)).astype(BF16)
@@ -147,7 +145,8 @@
     grad_ref[...] = grad
     grad_rows = dot(grad, panel, (1, 0))
     total, features = grad_rows.shape
-    cap = total // shards
+    shards, cap, _ = send_ref.shape
+    shards //= buckets
     width = features // buckets
     me = lax.axis_index("entity")
     lane = iota((total, LANES), 1)
@@ -161,33 +160,49 @@
             send_ref[b * shards + jnp.bitwise_xor(me, s)] = piece[s * cap : (s + 1) * cap]
 
 
-def panel_kernel(grad_ref, *refs):
-    fetched = jnp.concatenate([r[...] for r in refs[:-1]], axis=0)
-    refs[-1][0] = dot(grad_ref[...], fetched, (0, 0))
-
-
-def sum_kernel(width, got_ref, out_ref):
+def finish_kernel(width, got_ref, rel_grad_ref, grad_ref, *refs):
+    parts, (sums_hbm, panel_hbm, rel_hbm, out_ref, panel_ref, sems) = refs[:-6], refs[-6:]
+    fetched = jnp.concatenate([r[...] for r in parts], axis=0)
+    moves = [pltpu.make_async_copy(rel_grad_ref, rel_hbm, sems.at[0])]
+    moves[0].start()
+    features = fetched.shape[1]
+    half = features // 2
+    for i in range(2):
+        at = pl.ds(i * half, half)
+        panel_ref[at] = dot(grad_ref[:, i * half : (i + 1) * half], fetched, (0, 0))
+        moves.append(pltpu.make_async_copy(panel_ref.at[at], panel_hbm.at[0, at], sems.at[1 + i]))
+        moves[-1].start()
     devices, cap, _ = got_ref.shape
     rows = out_ref.shape[1]
     step = min(devices, 512 // cap)
+    count = step * cap
 
     def part(i):
-        got = got_ref[pl.ds(i * step, step)].reshape(step * cap, LANES)
-        wide = got.astype(F32)
-        column = (wide[:, 64:65] * DIGIT + wide[:, 96:97]).astype(I32)
-        hot = (column == iota((step * cap, rows), 1)).astype(F32).astype(BF16)
-        return dot(jnp.transpose(wide)[:width].astype(BF16), hot, (1, 0))
-
-    if devices == step:
-        out_ref[...] = part(0)
-    else:
-        out_ref[...] = jnp.zeros_like(out_ref)
-
-        def add(i, _):
-            out_ref[...] += part(i)
+        flat = jnp.transpose(got_ref[pl.ds(i * step, step)].reshape(count, LANES).astype(F32))
+        values = flat[:width].astype(BF16)
+        high, low = flat[64:65], flat[96:97]
+        hot = (low.astype(I32) == iota((DIGIT, count), 0)).astype(F32).astype(BF16)
+        kept = [values * (high == float(h)).astype(F32).astype(BF16) for h in range(rows // DIGIT)]
+        return dot(jnp.concatenate(kept, axis=0), hot, (1, 1))
+
+    def store(sums, add):
+        for h in range(rows // DIGIT):
+            piece = sums[h * width : (h + 1) * width]
+            at = slice(h * DIGIT, (h + 1) * DIGIT)
+            out_ref[:, at] = out_ref[:, at] + piece if add else piece
+
+    store(part(0), False)
+    if devices > step:
+
+        def more(i, _):
+            store(part(i), True)
             return 0
 
-        lax.fori_loop(0, devices // step, add, 0)
+        lax.fori_loop(1, devices // step, more, 0)
+    moves.append(pltpu.make_async_copy(out_ref, sums_hbm, sems.at[3]))
+    moves[-1].start()
+    for move in moves:
+        move.wait()
 
 
 def body(ent_table, panels, rel_vecs, head_slots, tail_slots, negatives, requests, block_count):
@@ -208,7 +223,8 @@
         return out(x.shape, x.dtype)
 
     vmem, hbm = pltpu.VMEM, pltpu.HBM
-    asked = [swap(requests, s) for s in range(1, shards)]
+    asked = [swap(requests, s) for s in range(3, shards, 2)]
+    other = swap(ent_table, 1)
     edges, pairs, rows, own, table, panel, rel = call(
         prepare_kernel,
         [pltpu.SMEM] + [hbm] * 7,
@@ -227,22 +243,30 @@
             for x in (head_slots, tail_slots, negatives, requests, ent_table, panels, rel_vecs)
         ]
     )
-    found = call(pick_kernel, [vmem] * (1 + shards), [out((cap, features), BF16)] * shards)(table, own, *asked)
-    parts = [found[0]] + [swap(found[s], s) for s in range(1, shards)]
+
+    def pick(first, ids):
+        kernel = functools.partial(pick_kernel, first)
+        return call(kernel, [vmem] * 3, [out((2 * cap, features), BF16)])(table, other, ids)[0]
+
+    found = [pick(1, ids) for ids in asked]
+    parts = [pick(0, own)] + [swap(x, 2 * c + 3) for c, x in enumerate(found)]
     send, grad, rel_grad = call(
         lambda *refs: terms_kernel(buckets, negatives.shape[2], *refs),
-        [vmem] * (5 + shards),
+        [vmem] * (5 + len(parts)),
         [out((buckets * shards, cap, LANES), BF16), out((total, features), BF16), out((1, features))],
     )(panel, rel, edges, pairs, rows, *parts)
     got = lax.all_to_all(send, ("bucket", "entity"), split_axis=0, concat_axis=0, tiled=True)
-    [panel_grad] = call(
-        panel_kernel,
-        [vmem] * (1 + shards),
-        [out((1, features, features))],
-        flops=2 * total * features * features,
-        nbytes=4 * features * features,
-    )(grad, *parts)
-    [ent_grad] = call(lambda *refs: sum_kernel(width, *refs), [vmem], [out((width, shard_rows))])(got)
+    ent_grad, panel_grad, rel_grad = call(
+        functools.partial(finish_kernel, width),
+        [vmem] * (3 + len(parts)),
+        [out((width, shard_rows)), out((1, features, features)), out((1, features))],
+        [
+            pltpu.VMEM((width, shard_rows), F32),
+            pltpu.VMEM((features, features), F32),
+            pltpu.SemaphoreType.DMA((4,)),
+        ],
+        hbm,
+    )(got, rel_grad, grad, *parts)
     return ent_grad.T, panel_grad, rel_grad
 
 

time: 29 us -> 25.7 us (0.89)
  blocking collectives: 0 us -> 13.3 us
  waiting for transfers between devices: 10.5 us -> 1.97 us
  starting transfers between devices: 10.9 us -> 4.21 us
  Pallas kernels: 6.03 us -> 4.7 us
    all_to_all x0 -> x1, blocking collectives: none -> 13.3 us  [body(): lax.all_to_all(send, ('bucket', 'entity'), split_axis=0, concat_axis=0, t...]
    all_to_all x1 -> x0, waiting for transfers between devices: 6.94 us -> none  [body(): lax.all_to_all(send, ('bucket', 'entity'), split_axis=0, concat_axis=0, t...]
    all_to_all x1 -> x0, starting transfers between devices: 5.75 us -> none  [body(): lax.all_to_all(send, ('bucket', 'entity'), split_axis=0, concat_axis=0, t...]
    ppermute x6 -> x3, waiting for transfers between devices: 3.55 us -> 1.97 us  [swap(): return lax.ppermute(x, 'entity', [(i, i ^ s) for i in range(shards)])]
    ppermute x6 -> x3, starting transfers between devices: 5.13 us -> 4.21 us  [swap(): return lax.ppermute(x, 'entity', [(i, i ^ s) for i in range(shards)])]
    pallas_call x3, Pallas kernels: 2.95 us -> 2.28 us  [the longest x1 1.4 us: body(): call(functools.partial(finish_kernel, width), [vmem] * (3 + len(parts)),...]
    pallas_call x1, Pallas kernels: 1.58 us -> 0.92 us  [body(): call(lambda *refs: terms_kernel(buckets, negatives.shape[2], *refs), [vme...]
  transfers between devices with their start and end apart: 7 -> 3, of which waited for: 3 -> 1; matrix products, arithmetic and copies ran while one was open for 0% -> 0% of each run, Pallas kernels for 10% -> 8%
where the time goes in v3:
time: 25.7 us; the launch traced here: 25.5 us
  blocking collectives  13.3 us (52%)
  Pallas kernels  4.7 us (18%)
  starting transfers between devices  4.21 us (16%)
  waiting for transfers between devices  1.97 us (8%)
  between operations  1.32 us (5%)
    all_to_all x1, blocking collectives, body(): lax.all_to_all(send, ('bucket', 'entity'), split_axis=0, concat_axis=0, t...  13.3 us
    ppermute x3, starting transfers between devices, swap(): return lax.ppermute(x, 'entity', [(i, i ^ s) for i in range(shards)])  4.21 us
    ppermute x3, waiting for transfers between devices, swap(): return lax.ppermute(x, 'entity', [(i, i ^ s) for i in range(shards)])  1.97 us
    pallas_call x1, Pallas kernels, body(): call(prepare_kernel, [pltpu.SMEM] + [hbm] * 7, [out((total, total)), out(...  1.5 us
    pallas_call x1, Pallas kernels, body(): call(functools.partial(finish_kernel, width), [vmem] * (3 + len(parts)),...  1.4 us
    pallas_call x1, Pallas kernels, body(): call(lambda *refs: terms_kernel(buckets, negatives.shape[2], *refs), [vme...  0.92 us
    pallas_call x2, Pallas kernels, pick(): call(kernel, [vmem] * 3, [out((2 * cap, features), BF16)])  0.87 us
  transfers between devices with their start and end apart: 3, of which 1 were waited for; matrix products, arithmetic and copies ran while one was open for 0% of the time, Pallas kernels for 8%

profile of v3, /device:TPU:0, one launch (start us, length us, event | category | flops | bytes accessed | tf_op | source)
XLA Modules:
  0.0 25.5 jit_solution(11907135338354385954)
XLA Ops:
  0.6 0.5 %collective-permute-start = (bf16[1024,512]{1,0:T(8,128)(2,1)}, bf16[1024,512]{1,0:T(8,128)(2,1)S(1)}, u32[]{:S(2)}, u32[]{:S(2)}) collective-permute-start(bf16[1024,512]{1,0:T(8,128)(2,1)} %table_hbm.1), channel_id=1, source_target_pairs={{0,1},{1,0},{2,3},{3,2},{4,5},{5,4},{6,7},{7,6},{8,9},{9,8},{10,11... | collective-permute-start | bytes 3145736 | tf_op jit(solution)/shard_map/ppermute | solution.py:217
  1.2 2.6 %collective-permute-start.1 = (s32[1,4,16]{2,1,0:T(4,128)}, s32[1,4,16]{2,1,0:T(4,128)S(1)}, u32[]{:S(2)}, u32[]{:S(2)}) collective-permute-start(s32[1,4,16]{2,1,0:T(4,128)} %req_hbm.1), channel_id=1, source_target_pairs={{0,3},{1,2},{2,1},{3,0},{4,7},{5,6},{6,5},{7,4},{8,11},{9,10},{10,... | collective-permute-start | bytes 776 | tf_op jit(solution)/shard_map/ppermute | solution.py:217
  4.4 1.5 %shard_map.103 = (f32[64,64]{1,0:T(8,128)S(1)}, f32[64,64]{1,0:T(8,128)S(1)}, f32[64,128]{1,0:T(8,128)S(1)}, s32[1,4,16]{2,1,0:T(4,128)S(1)}, bf16[1024,512]{1,0...) custom-call(s32[1]{0:T(128)S(6)} %copy.11.count_ref, s32[1,2,128]{2,1,0:T(2,128)} %head_hbm.1, ...), custom_call_target="tpu_custom_call" | custom-call | tf_op jit(solution)/shard_map/pallas_call | solution.py:228
  6.0 0.0 collective-permute-done.1.asked_ref
  6.0 0.0 collective-permute-done.other_ref
  6.0 0.4 %shard_map.105 = bf16[32,512]{1,0:T(8,128)(2,1)S(1)} custom-call(bf16[1024,512]{1,0:T(8,128)(2,1)S(1)} %get-tuple-element.21.near_ref, bf16[1024,512]{1,0:T(8,128)(2,1)S(1)} %collective-permute-done.other_ref, s32[1,4,16]{2,1,0:T(4,128)S(1)} %collective-permute-done.1.asked_ref), custom_call_target="tpu_custom_call" | custom-call | tf_op jit(solution)/shard_map/pallas_call | solution.py:249
  6.4 1.1 %collective-permute-start.2 = (bf16[32,512]{1,0:T(8,128)(2,1)S(1)}, bf16[32,512]{1,0:T(8,128)(2,1)S(1)}, u32[]{:S(2)}, u32[]{:S(2)}) collective-permute-start(bf16[32,512]{1,0:T(8,128)(2,1)S(1)} %shard_map.105), channel_id=1, source_target_pairs={{0,3},{1,2},{2,1},{3,0},{4,7},{5,6},{6,5},{7,4},{8,11},{9,10},{10,... | collective-permute-start | bytes 98312 | tf_op jit(solution)/shard_map/ppermute | solution.py:217
  7.5 0.4 %shard_map.104.refs_5_.refs_0_ = bf16[32,512]{1,0:T(8,128)(2,1)S(1)} custom-call(bf16[1024,512]{1,0:T(8,128)(2,1)S(1)} %get-tuple-element.21.near_ref, bf16[1024,512]{1,0:T(8,128)(2,1)S(1)} %collective-permute-done.other_ref, s32[1,4,16]{2,1,0:T(4,128)S(1)} %get-tuple-element.22.asked_ref), custom_call_target="tpu_custom_call" | custom-call | tf_op jit(solution)/shard_map/pallas_call | solution.py:249
  7.9 2.0 %collective-permute-done.2.refs_6_.refs_1_ = bf16[32,512]{1,0:T(8,128)(2,1)S(1)} collective-permute-done((bf16[32,512]{1,0:T(8,128)(2,1)S(1)}, bf16[32,512]{1,0:T(8,128)(2,1)S(1)}, u32[]{:S(2)}, u32[]{:S(2)}) %collective-permute-start.2) | collective-permute-done | bytes 32800 | tf_op jit(solution)/shard_map/ppermute | solution.py:217
  9.9 0.9 %shard_map.106 = (bf16[32,16,128]{2,1,0:T(8,128)(2,1)S(1)}, bf16[64,512]{1,0:T(8,128)(2,1)S(1)}, f32[1,512]{1,0:T(1,128)S(1)}) custom-call(bf16[1,512,512]{2,1,0:T(8,128)(2,1)S(1)} %get-tuple-element.16.refs_0_, bf16[1,512]{1,0:T(2,128)(2,1)S(1)} %get-tuple-element.17.refs_1_, f32[64,64]{1,0:T(8,128)S(1)} %get-tuple-element.18.refs_2_, ...), custom_call_target="tpu_custom_call" | custom-call | tf_op jit(solution)/shard_map/pallas_call | solution.py:253
  10.8 13.3 %all_to_all.5.got_ref = bf16[32,16,128]{2,1,0:T(8,128)(2,1)S(1)} all-to-all(bf16[32,16,128]{2,1,0:T(8,128)(2,1)S(1)} %get-tuple-element.23), channel_id=1, replica_groups=mesh['bucket'=8,'entity'=4] {'bucket','entity'}, dimensions={0} | all-to-all | bytes 262144 | tf_op jit(solution)/shard_map/all_to_all | solution.py:258
  24.1 1.4 %shard_map.107 = (f32[64,1024]{1,0:T(8,128)}, f32[1,512,512]{2,1,0:T(8,128)}, f32[1,512]{1,0:T(1,128)}) custom-call(bf16[32,16,128]{2,1,0:T(8,128)(2,1)S(1)} %all_to_all.5.got_ref, f32[1,512]{1,0:T(1,128)S(1)} %get-tuple-element.24.rel_grad_ref, bf16[64,512]{1,0:T(8,128)(2,1)S(1)} %get-tuple-element.25.grad_ref, ...), custom_call_target="tpu_custom_call" | custom-call | tf_op jit(solution)/shard_map/pallas_call | solution.py:259
Async XLA Ops:
  0.6 5.3 %collective-permute-start = (bf16[1024,512]{1,0:T(8,128)(2,1)}, bf16[1024,512]{1,0:T(8,128)(2,1)S(1)}, u32[]{:S(2)}, u32[]{:S(2)}) collective-permute-start(bf16[1024,512]{1,0:T(8,128)(2,1)} %table_hbm.1), channel_id=1, source_target_pairs={{0,1},{1,0},{2,3},{3,2},{4,5},{5,4},{6,7},{7,6},{8,9},{9,8},{10,11... | collective-permute-start | bytes 3145736 | tf_op jit(solution)/shard_map/ppermute | solution.py:217
  1.2 4.8 %collective-permute-start.1 = (s32[1,4,16]{2,1,0:T(4,128)}, s32[1,4,16]{2,1,0:T(4,128)S(1)}, u32[]{:S(2)}, u32[]{:S(2)}) collective-permute-start(s32[1,4,16]{2,1,0:T(4,128)} %req_hbm.1), channel_id=1, source_target_pairs={{0,3},{1,2},{2,1},{3,0},{4,7},{5,6},{6,5},{7,4},{8,11},{9,10},{10,... | collective-permute-start | bytes 776 | tf_op jit(solution)/shard_map/ppermute | solution.py:217
  6.4 3.5 %collective-permute-start.2 = (bf16[32,512]{1,0:T(8,128)(2,1)S(1)}, bf16[32,512]{1,0:T(8,128)(2,1)S(1)}, u32[]{:S(2)}, u32[]{:S(2)}) collective-permute-start(bf16[32,512]{1,0:T(8,128)(2,1)S(1)} %shard_map.105), channel_id=1, source_target_pairs={{0,3},{1,2},{2,1},{3,0},{4,7},{5,6},{6,5},{7,4},{8,11},{9,10},{10,... | collective-permute-start | bytes 98312 | tf_op jit(solution)/shard_map/ppermute | solution.py:217

commit v4 on v3

--- a/solution.py
+++ b/solution.py
@@ -9,6 +9,7 @@
 
 MARGIN = 2.0
 LANES = 128
+FOLD = 4
 DIGIT = 256
 F32 = jnp.float32
 BF16 = jnp.bfloat16
@@ -34,11 +35,6 @@
 def flip(column):
     n = column.shape[0]
     return jnp.sum(jnp.where(iota((n, n), 0) == iota((n, n), 1), column, 0.0), axis=0, keepdims=True)
-
-
-def flip_back(row):
-    n = row.shape[1]
-    return jnp.sum(jnp.where(iota((n, n), 0) == iota((n, n), 1), row, 0.0), axis=1, keepdims=True)
 
 
 def call(kernel, ins, outs, scratch=(), space=pltpu.VMEM):
@@ -81,8 +77,9 @@
     blocks, edge = head_ref.shape[1:]
     negs = neg_ref.shape[2]
     live_blocks = count_ref[0]
-    edges = jnp.zeros((total, total), F32)
-    pairs = jnp.zeros((total, total), F32)
+    edges = jnp.zeros((2 * total, 2 * total), F32)
+    pairs = jnp.zeros((total, 2 * total), F32)
+    left = iota(pairs.shape, 1) < total
     edge_slot = jnp.bitwise_xor(iota((total, edge), 0), me * cap)
     neg_slot = jnp.bitwise_xor(iota((total, negs), 0), me * cap)
     for j in range(blocks):
@@ -90,16 +87,22 @@
         head = (head_ref[0, j : j + 1, :] == edge_slot).astype(F32) * live
         tail = (tail_ref[0, j : j + 1, :] == edge_slot).astype(F32)
         neg = (neg_ref[0, j : j + 1, :] == neg_slot).astype(F32)
-        edges += dot(head.astype(BF16), tail.astype(BF16), (1, 1))
+        ends = jnp.concatenate([head, tail], axis=0).astype(BF16)
+        edges += dot(ends, ends, (1, 1))
         heads = jnp.sum(head, axis=1, keepdims=True)
-        negatives = dot(jnp.ones((8, negs), BF16), neg.astype(BF16), (1, 1))[0:1]
-        pairs += heads * negatives
-    edges_ref[...] = edges
+        others = jnp.sum(neg, axis=1, keepdims=True)
+        pairs += jnp.where(left, others, heads) * flip(jnp.concatenate([heads, others], axis=0))
+    edges_ref[...] = jnp.where(left, edges[total:], edges[:total])
     pairs_ref[...] = pairs
-    column = to_column([req_ref[0, pl.ds(jnp.bitwise_xor(me, s), 1), :] for s in range(shards)])
-    high = jnp.floor(column * (1.0 / DIGIT))
-    low = column - high * DIGIT
-    rows_ref[...] = jnp.where(iota((total, LANES), 1) < 96, high, low)
+    numbers = jnp.concatenate([req_ref[0, pl.ds(jnp.bitwise_xor(me, s), 1), :] for s in range(shards)], axis=0)
+    lane = iota((shards, LANES), 1)
+    span = LANES // (cap // FOLD)
+    for i in range(FOLD):
+        spread = jnp.zeros((shards, LANES), I32)
+        for k in range(cap // FOLD):
+            spread = jnp.where(lane // span == k, numbers[:, k * FOLD + i : k * FOLD + i + 1], spread)
+        digit = jnp.where(lane % span < span // 2, spread // DIGIT, spread % DIGIT)
+        rows_ref[:, i, :] = digit.astype(F32)
     for move in moves[4:]:
         move.wait()
 
@@ -114,21 +117,29 @@
         out_ref[at : at + cap] = dot(hot, table_ref[...], (1, 0)).astype(BF16)
 
 
+def turn_kernel(panel_ref, out_ref):
+    out_ref[...] = jnp.transpose(panel_ref[0])
+
+
 def terms_kernel(buckets, negs, *refs):
-    panel_ref, rel_ref, edges_ref, pairs_ref, rows_ref = refs[:5]
+    panel_ref, turned_ref, rel_ref, edges_ref, pairs_ref, rows_ref = refs[:6]
     send_ref, grad_ref, rel_grad_ref = refs[-3:]
-    parts = refs[5:-3]
-    fetched = jnp.concatenate([r[...] for r in parts], axis=0)
-    panel = panel_ref[0]
-    proj = dot(fetched, panel, (1, 1)).astype(BF16)
+    fetched = jnp.concatenate([r[...] for r in refs[6:-3]], axis=0)
+    proj = dot(fetched, turned_ref[...], (1, 0)).astype(BF16)
     proj_f = proj.astype(F32)
     centers = (proj_f + rel_ref[...].astype(F32)).astype(BF16)
     center_f = centers.astype(F32)
-    cross = dot(centers, proj, (1, 1))
+    total, features = proj.shape
+    points = jnp.concatenate([centers, proj], axis=0)
+    gram = dot(points, points, (1, 1))
+    norms = jnp.concatenate(
+        [jnp.sum(x * x, axis=1, keepdims=True) for x in (center_f, proj_f)], axis=0
+    )
+    left = iota((total, 2 * total), 1) < total
     dist = (
-        jnp.sum(center_f * center_f, axis=1, keepdims=True)
-        + flip(jnp.sum(proj_f * proj_f, axis=1, keepdims=True))
-        - 2.0 * cross
+        jnp.where(left, norms[total:], norms[:total])
+        + flip(norms)
+        - 2.0 * jnp.where(left, gram[total:], gram[:total])
     )
     pos = edges_ref[...] * jax.nn.sigmoid(dist - MARGIN)
     neg = -jax.nn.sigmoid(MARGIN - dist) * (1.0 / negs)
@@ -136,28 +147,33 @@
     rounded = pos + pairs_ref[...] * neg.astype(BF16).astype(F32)
     high = rounded.astype(BF16)
     low = (rounded - high.astype(F32)).astype(BF16)
-    row_sum = jnp.sum(exact, axis=1, keepdims=True)
-    col_sum = flip_back(jnp.sum(exact, axis=0, keepdims=True))
-    grad_center = 2.0 * (row_sum * center_f - dot(high, proj, (1, 0)) - dot(low, proj, (1, 0)))
-    grad_other = 2.0 * (col_sum * proj_f - dot(high, centers, (0, 0)) - dot(low, centers, (0, 0)))
-    rel_grad_ref[...] = jnp.sum(grad_center, axis=0, keepdims=True)
-    grad = (grad_center + grad_other).astype(BF16)
+    mixed = dot(jnp.concatenate([high, low], axis=0), points, (1, 0))
+    from_centers = jnp.sum(jnp.where(left, 0.0, exact), axis=1, keepdims=True) * center_f
+    from_others = jnp.sum(jnp.where(left, exact, 0.0), axis=1, keepdims=True) * proj_f
+    grad = (2.0 * (from_centers + from_others - mixed[:total] - mixed[total:])).astype(BF16)
     grad_ref[...] = grad
-    grad_rows = dot(grad, panel, (1, 0))
-    total, features = grad_rows.shape
-    shards, cap, _ = send_ref.shape
-    shards //= buckets
+    grad_rows = dot(grad, panel_ref[0], (1, 0))
+    devices, tiles, _, _ = send_ref.shape
+    shards = devices // buckets
+    tiles -= 1
     width = features // buckets
     me = lax.axis_index("entity")
     lane = iota((total, LANES), 1)
+    rows = rows_ref[...].astype(BF16)
     for b in range(buckets):
         block, offset = divmod(b * width, LANES)
         piece = grad_rows[:, block * LANES : (block + 1) * LANES]
-        if offset:
-            piece = pltpu.roll(piece, LANES - offset, 1)
-        piece = jnp.where(lane < width, piece, rows_ref[...]).astype(BF16)
+        near = pltpu.roll(piece, LANES - offset, 1) if offset else piece
+        far = pltpu.roll(piece, (LANES + LANES // 2 - offset) % LANES, 1) if offset != LANES // 2 else piece
+        far = pltpu.roll(far, total - FOLD, 0)
+        piece = jnp.where(lane < LANES // 2, near, far).reshape(total // (2 * FOLD), 2 * FOLD, LANES)
+        piece = piece[:, :FOLD].astype(BF16)
         for s in range(shards):
-            send_ref[b * shards + jnp.bitwise_xor(me, s)] = piece[s * cap : (s + 1) * cap]
+            to = b * shards + jnp.bitwise_xor(me, s)
+            send_ref[to, :tiles] = piece[s * tiles : (s + 1) * tiles]
+            send_ref[to, tiles] = rows[s]
+    from_others = jnp.sum(jnp.where(left, rounded, 0.0), axis=1, keepdims=True) * proj_f
+    rel_grad_ref[...] = 2.0 * jnp.sum(from_centers - from_others, axis=0, keepdims=True)
 
 
 def finish_kernel(width, got_ref, rel_grad_ref, grad_ref, *refs):
@@ -172,16 +188,20 @@
         panel_ref[at] = dot(grad_ref[:, i * half : (i + 1) * half], fetched, (0, 0))
         moves.append(pltpu.make_async_copy(panel_ref.at[at], panel_hbm.at[0, at], sems.at[1 + i]))
         moves[-1].start()
-    devices, cap, _ = got_ref.shape
+    devices, tiles, _, _ = got_ref.shape
+    tiles -= 1
     rows = out_ref.shape[1]
-    step = min(devices, 512 // cap)
-    count = step * cap
+    step = min(devices, 32)
+    span = LANES // (2 * tiles)
 
     def part(i):
-        flat = jnp.transpose(got_ref[pl.ds(i * step, step)].reshape(count, LANES).astype(F32))
-        values = flat[:width].astype(BF16)
-        high, low = flat[64:65], flat[96:97]
-        hot = (low.astype(I32) == iota((DIGIT, count), 0)).astype(F32).astype(BF16)
+        got = got_ref[pl.ds(i * step, step)].astype(F32)
+        turned = [jnp.transpose(got[:, k].reshape(step * FOLD, LANES)) for k in range(tiles + 1)]
+        starts = [(t, at) for t in turned[:tiles] for at in (0, LANES // 2)]
+        values = jnp.concatenate([t[at : at + width] for t, at in starts], axis=1).astype(BF16)
+        digits = [turned[tiles][k * span // 2 : k * span // 2 + 1] for k in range(4 * tiles)]
+        high, low = jnp.concatenate(digits[0::2], axis=1), jnp.concatenate(digits[1::2], axis=1)
+        hot = (low.astype(I32) == iota((DIGIT, low.shape[1]), 0)).astype(F32).astype(BF16)
         kept = [values * (high == float(h)).astype(F32).astype(BF16) for h in range(rows // DIGIT)]
         return dot(jnp.concatenate(kept, axis=0), hot, (1, 1))
 
@@ -228,7 +248,7 @@
     edges, pairs, rows, own, table, panel, rel = call(
         prepare_kernel,
         [pltpu.SMEM] + [hbm] * 7,
-        [out((total, total)), out((total, total)), out((total, LANES))]
+        [out((total, 2 * total)), out((total, 2 * total)), out((shards, FOLD, LANES))]
         + [like(x) for x in (requests, ent_table, panels, rel_vecs)],
         [
             pltpu.VMEM(head_slots.shape, I32),
@@ -250,11 +270,12 @@
 
     found = [pick(1, ids) for ids in asked]
     parts = [pick(0, own)] + [swap(x, 2 * c + 3) for c, x in enumerate(found)]
+    [turned] = call(turn_kernel, [vmem], [out((features, features), BF16)])(panel)
     send, grad, rel_grad = call(
         lambda *refs: terms_kernel(buckets, negatives.shape[2], *refs),
-        [vmem] * (5 + len(parts)),
-        [out((buckets * shards, cap, LANES), BF16), out((total, features), BF16), out((1, features))],
-    )(panel, rel, edges, pairs, rows, *parts)
+        [vmem] * (6 + len(parts)),
+        [out((buckets * shards, cap // (2 * FOLD) + 1, FOLD, LANES), BF16), out((total, features), BF16), out((1, features))],
+    )(panel, turned, rel, edges, pairs, rows, *parts)
     got = lax.all_to_all(send, ("bucket", "entity"), split_axis=0, concat_axis=0, tiled=True)
     ent_grad, panel_grad, rel_grad = call(
         functools.partial(finish_kernel, width),

time: 25.7 us -> 25.3 us (0.984)
  blocking collectives: 13.3 us -> 12.9 us
    all_to_all x1, blocking collectives: 13.3 us -> 12.9 us  [body(): lax.all_to_all(send, ('bucket', 'entity'), split_axis=0, concat_axis=0, t...]
    pallas_call x1 -> x2, Pallas kernels: 1.5 us -> 1.68 us  [the longest x1 1.5 us: body(): call(prepare_kernel, [pltpu.SMEM] + [hbm] * 7, [out((total, 2 * total)),...]
where the time goes in v4:
time: 25.3 us; the launch traced here: 25.1 us
  blocking collectives  12.9 us (51%)
  Pallas kernels  4.88 us (19%)
  starting transfers between devices  4.21 us (17%)
  waiting for transfers between devices  1.78 us (7%)
  between operations  1.33 us (5%)
    all_to_all x1, blocking collectives, body(): lax.all_to_all(send, ('bucket', 'entity'), split_axis=0, concat_axis=0, t...  12.9 us
    ppermute x3, starting transfers between devices, swap(): return lax.ppermute(x, 'entity', [(i, i ^ s) for i in range(shards)])  4.21 us
    ppermute x3, waiting for transfers between devices, swap(): return lax.ppermute(x, 'entity', [(i, i ^ s) for i in range(shards)])  1.78 us
    pallas_call x1, Pallas kernels, body(): call(prepare_kernel, [pltpu.SMEM] + [hbm] * 7, [out((total, 2 * total)),...  1.5 us
    pallas_call x1, Pallas kernels, body(): call(functools.partial(finish_kernel, width), [vmem] * (3 + len(parts)),...  1.44 us
    pallas_call x1, Pallas kernels, body(): call(lambda *refs: terms_kernel(buckets, negatives.shape[2], *refs), [vme...  0.89 us
    pallas_call x2, Pallas kernels, pick(): call(kernel, [vmem] * 3, [out((2 * cap, features), BF16)])  0.88 us
  transfers between devices with their start and end apart: 3, of which 1 were waited for; matrix products, arithmetic and copies ran while one was open for 0% of the time, Pallas kernels for 8%

profile of v4, /device:TPU:0, one launch (start us, length us, event | category | flops | bytes accessed | tf_op | source)
XLA Modules:
  0.0 25.1 jit_solution(3893845721839461262)
XLA Ops:
  0.6 0.5 %collective-permute-start = (bf16[1024,512]{1,0:T(8,128)(2,1)}, bf16[1024,512]{1,0:T(8,128)(2,1)S(1)}, u32[]{:S(2)}, u32[]{:S(2)}) collective-permute-start(bf16[1024,512]{1,0:T(8,128)(2,1)} %table_hbm.1), channel_id=1, source_target_pairs={{0,1},{1,0},{2,3},{3,2},{4,5},{5,4},{6,7},{7,6},{8,9},{9,8},{10,11... | collective-permute-start | bytes 3145736 | tf_op jit(solution)/shard_map/ppermute | solution.py:237
  1.2 2.6 %collective-permute-start.1 = (s32[1,4,16]{2,1,0:T(4,128)}, s32[1,4,16]{2,1,0:T(4,128)S(1)}, u32[]{:S(2)}, u32[]{:S(2)}) collective-permute-start(s32[1,4,16]{2,1,0:T(4,128)} %req_hbm.1), channel_id=1, source_target_pairs={{0,3},{1,2},{2,1},{3,0},{4,7},{5,6},{6,5},{7,4},{8,11},{9,10},{10,... | collective-permute-start | bytes 776 | tf_op jit(solution)/shard_map/ppermute | solution.py:237
  4.4 1.5 %shard_map.103 = (f32[64,128]{1,0:T(8,128)S(1)}, f32[64,128]{1,0:T(8,128)S(1)}, f32[4,4,128]{2,1,0:T(4,128)S(1)}, s32[1,4,16]{2,1,0:T(4,128)S(1)}, bf16[1024,512...) custom-call(s32[1]{0:T(128)S(6)} %copy.11.count_ref, s32[1,2,128]{2,1,0:T(2,128)} %head_hbm.1, ...), custom_call_target="tpu_custom_call" | custom-call | tf_op jit(solution)/shard_map/pallas_call | solution.py:248
  6.0 0.0 collective-permute-done.1.asked_ref
  6.0 0.0 collective-permute-done.other_ref
  6.0 0.4 %shard_map.106 = bf16[32,512]{1,0:T(8,128)(2,1)S(1)} custom-call(bf16[1024,512]{1,0:T(8,128)(2,1)S(1)} %get-tuple-element.21.near_ref, bf16[1024,512]{1,0:T(8,128)(2,1)S(1)} %collective-permute-done.other_ref, s32[1,4,16]{2,1,0:T(4,128)S(1)} %collective-permute-done.1.asked_ref), custom_call_target="tpu_custom_call" | custom-call | tf_op jit(solution)/shard_map/pallas_call | solution.py:269
  6.4 1.1 %collective-permute-start.2 = (bf16[32,512]{1,0:T(8,128)(2,1)S(1)}, bf16[32,512]{1,0:T(8,128)(2,1)S(1)}, u32[]{:S(2)}, u32[]{:S(2)}) collective-permute-start(bf16[32,512]{1,0:T(8,128)(2,1)S(1)} %shard_map.106), channel_id=1, source_target_pairs={{0,3},{1,2},{2,1},{3,0},{4,7},{5,6},{6,5},{7,4},{8,11},{9,10},{10,... | collective-permute-start | bytes 98312 | tf_op jit(solution)/shard_map/ppermute | solution.py:237
  7.5 0.2 shard_map.104.refs_1_
  7.7 0.4 %shard_map.105.refs_6_.refs_0_ = bf16[32,512]{1,0:T(8,128)(2,1)S(1)} custom-call(bf16[1024,512]{1,0:T(8,128)(2,1)S(1)} %get-tuple-element.21.near_ref, bf16[1024,512]{1,0:T(8,128)(2,1)S(1)} %collective-permute-done.other_ref, s32[1,4,16]{2,1,0:T(4,128)S(1)} %get-tuple-element.22.asked_ref), custom_call_target="tpu_custom_call" | custom-call | tf_op jit(solution)/shard_map/pallas_call | solution.py:269
  8.1 1.8 %collective-permute-done.2.refs_7_.refs_1_ = bf16[32,512]{1,0:T(8,128)(2,1)S(1)} collective-permute-done((bf16[32,512]{1,0:T(8,128)(2,1)S(1)}, bf16[32,512]{1,0:T(8,128)(2,1)S(1)}, u32[]{:S(2)}, u32[]{:S(2)}) %collective-permute-start.2) | collective-permute-done | bytes 32800 | tf_op jit(solution)/shard_map/ppermute | solution.py:237
  9.9 0.9 %shard_map.107 = (bf16[32,3,4,128]{3,2,1,0:T(4,128)(2,1)S(1)}, bf16[64,512]{1,0:T(8,128)(2,1)S(1)}, f32[1,512]{1,0:T(1,128)S(1)}) custom-call(bf16[1,512,512]{2,1,0:T(8,128)(2,1)S(1)} %get-tuple-element.16.panel_ref.refs_0_, bf16[512,512]{1,0:T(8,128)(2,1)S(1)} %shard_map.104.refs_1_, bf16[1,512]{1,0:T(2,128)(2,1)S(1)} %get-tuple-element.17.refs_2_, ...), custom_call_target="tpu_custom_call" | custom-call | tf_op jit(solution)/shard_map/pallas_call | solution.py:274
  10.8 12.9 %all_to_all.5.got_ref = bf16[32,3,4,128]{3,2,1,0:T(4,128)(2,1)S(1)} all-to-all(bf16[32,3,4,128]{3,2,1,0:T(4,128)(2,1)S(1)} %get-tuple-element.23), channel_id=1, replica_groups=mesh['bucket'=8,'entity'=4] {'bucket','entity'}, dimensions={0} | all-to-all | bytes 196608 | tf_op jit(solution)/shard_map/all_to_all | solution.py:279
  23.6 1.4 %shard_map.108 = (f32[64,1024]{1,0:T(8,128)}, f32[1,512,512]{2,1,0:T(8,128)}, f32[1,512]{1,0:T(1,128)}) custom-call(bf16[32,3,4,128]{3,2,1,0:T(4,128)(2,1)S(1)} %all_to_all.5.got_ref, f32[1,512]{1,0:T(1,128)S(1)} %get-tuple-element.24.rel_grad_ref, bf16[64,512]{1,0:T(8,128)(2,1)S(1)} %get-tuple-element.25.grad_ref, ...), custom_call_target="tpu_custom_call" | custom-call | tf_op jit(solution)/shard_map/pallas_call | solution.py:280
Async XLA Ops:
  0.6 5.3 %collective-permute-start = (bf16[1024,512]{1,0:T(8,128)(2,1)}, bf16[1024,512]{1,0:T(8,128)(2,1)S(1)}, u32[]{:S(2)}, u32[]{:S(2)}) collective-permute-start(bf16[1024,512]{1,0:T(8,128)(2,1)} %table_hbm.1), channel_id=1, source_target_pairs={{0,1},{1,0},{2,3},{3,2},{4,5},{5,4},{6,7},{7,6},{8,9},{9,8},{10,11... | collective-permute-start | bytes 3145736 | tf_op jit(solution)/shard_map/ppermute | solution.py:237
  1.2 4.8 %collective-permute-start.1 = (s32[1,4,16]{2,1,0:T(4,128)}, s32[1,4,16]{2,1,0:T(4,128)S(1)}, u32[]{:S(2)}, u32[]{:S(2)}) collective-permute-start(s32[1,4,16]{2,1,0:T(4,128)} %req_hbm.1), channel_id=1, source_target_pairs={{0,3},{1,2},{2,1},{3,0},{4,7},{5,6},{6,5},{7,4},{8,11},{9,10},{10,... | collective-permute-start | bytes 776 | tf_op jit(solution)/shard_map/ppermute | solution.py:237
  6.4 3.5 %collective-permute-start.2 = (bf16[32,512]{1,0:T(8,128)(2,1)S(1)}, bf16[32,512]{1,0:T(8,128)(2,1)S(1)}, u32[]{:S(2)}, u32[]{:S(2)}) collective-permute-start(bf16[32,512]{1,0:T(8,128)(2,1)S(1)} %shard_map.106), channel_id=1, source_target_pairs={{0,3},{1,2},{2,1},{3,0},{4,7},{5,6},{6,5},{7,4},{8,11},{9,10},{10,... | collective-permute-start | bytes 98312 | tf_op jit(solution)/shard_map/ppermute | solution.py:237

commit v5 on v4

--- a/solution.py
+++ b/solution.py
@@ -123,7 +123,7 @@
 
 def terms_kernel(buckets, negs, *refs):
     panel_ref, turned_ref, rel_ref, edges_ref, pairs_ref, rows_ref = refs[:6]
-    send_ref, grad_ref, rel_grad_ref = refs[-3:]
+    send_ref, panel_grad_ref, rel_grad_ref = refs[-3:]
     fetched = jnp.concatenate([r[...] for r in refs[6:-3]], axis=0)
     proj = dot(fetched, turned_ref[...], (1, 0)).astype(BF16)
     proj_f = proj.astype(F32)
@@ -151,8 +151,8 @@
     from_centers = jnp.sum(jnp.where(left, 0.0, exact), axis=1, keepdims=True) * center_f
     from_others = jnp.sum(jnp.where(left, exact, 0.0), axis=1, keepdims=True) * proj_f
     grad = (2.0 * (from_centers + from_others - mixed[:total] - mixed[total:])).astype(BF16)
-    grad_ref[...] = grad
     grad_rows = dot(grad, panel_ref[0], (1, 0))
+    panel_grad_ref[...] = dot(grad, fetched, (0, 0))
     devices, tiles, _, _ = send_ref.shape
     shards = devices // buckets
     tiles -= 1
@@ -176,18 +176,13 @@
     rel_grad_ref[...] = 2.0 * jnp.sum(from_centers - from_others, axis=0, keepdims=True)
 
 
-def finish_kernel(width, got_ref, rel_grad_ref, grad_ref, *refs):
-    parts, (sums_hbm, panel_hbm, rel_hbm, out_ref, panel_ref, sems) = refs[:-6], refs[-6:]
-    fetched = jnp.concatenate([r[...] for r in parts], axis=0)
-    moves = [pltpu.make_async_copy(rel_grad_ref, rel_hbm, sems.at[0])]
-    moves[0].start()
-    features = fetched.shape[1]
-    half = features // 2
-    for i in range(2):
-        at = pl.ds(i * half, half)
-        panel_ref[at] = dot(grad_ref[:, i * half : (i + 1) * half], fetched, (0, 0))
-        moves.append(pltpu.make_async_copy(panel_ref.at[at], panel_hbm.at[0, at], sems.at[1 + i]))
-        moves[-1].start()
+def finish_kernel(width, got_ref, panel_ref, rel_grad_ref, sums_hbm, panel_hbm, rel_hbm, out_ref, sems):
+    moves = [
+        pltpu.make_async_copy(panel_ref, panel_hbm.at[0], sems.at[0]),
+        pltpu.make_async_copy(rel_grad_ref, rel_hbm, sems.at[1]),
+    ]
+    for move in moves:
+        move.start()
     devices, tiles, _, _ = got_ref.shape
     tiles -= 1
     rows = out_ref.shape[1]
@@ -219,7 +214,7 @@
             return 0
 
         lax.fori_loop(1, devices // step, more, 0)
-    moves.append(pltpu.make_async_copy(out_ref, sums_hbm, sems.at[3]))
+    moves.append(pltpu.make_async_copy(out_ref, sums_hbm, sems.at[2]))
     moves[-1].start()
     for move in moves:
         move.wait()
@@ -271,23 +266,22 @@
     found = [pick(1, ids) for ids in asked]
     parts = [pick(0, own)] + [swap(x, 2 * c + 3) for c, x in enumerate(found)]
     [turned] = call(turn_kernel, [vmem], [out((features, features), BF16)])(panel)
-    send, grad, rel_grad = call(
+    send, panel_grad, rel_grad = call(
         lambda *refs: terms_kernel(buckets, negatives.shape[2], *refs),
         [vmem] * (6 + len(parts)),
-        [out((buckets * shards, cap // (2 * FOLD) + 1, FOLD, LANES), BF16), out((total, features), BF16), out((1, features))],
+        [out((buckets * shards, cap // (2 * FOLD) + 1, FOLD, LANES), BF16), out((features, features)), out((1, features))],
     )(panel, turned, rel, edges, pairs, rows, *parts)
     got = lax.all_to_all(send, ("bucket", "entity"), split_axis=0, concat_axis=0, tiled=True)
     ent_grad, panel_grad, rel_grad = call(
         functools.partial(finish_kernel, width),
-        [vmem] * (3 + len(parts)),
+        [vmem] * 3,
         [out((width, shard_rows)), out((1, features, features)), out((1, features))],
         [
             pltpu.VMEM((width, shard_rows), F32),
-            pltpu.VMEM((features, features), F32),
-            pltpu.SemaphoreType.DMA((4,)),
+            pltpu.SemaphoreType.DMA((3,)),
         ],
         hbm,
-    )(got, rel_grad, grad, *parts)
+    )(got, panel_grad, rel_grad)
     return ent_grad.T, panel_grad, rel_grad
 
 

time: 25.3 us -> 25 us (0.988)
  Pallas kernels: 4.88 us -> 4.57 us
    pallas_call x1, Pallas kernels: 1.44 us -> 1.09 us  [body(): call(functools.partial(finish_kernel, width), [vmem] * 3, [out((width, sh...]
  transfers between devices with their start and end apart: 3 -> 3, of which waited for: 1 -> 1; matrix products, arithmetic and copies ran while one was open for 0% -> 0% of each run, Pallas kernels for 8% -> 9%
where the time goes in v5:
time: 25 us; the launch traced here: 24.8 us
  blocking collectives  12.9 us (52%)
  Pallas kernels  4.57 us (18%)
  starting transfers between devices  4.21 us (17%)
  waiting for transfers between devices  1.78 us (7%)
  between operations  1.32 us (5%)
    all_to_all x1, blocking collectives, body(): lax.all_to_all(send, ('bucket', 'entity'), split_axis=0, concat_axis=0, t...  12.9 us
    ppermute x3, starting transfers between devices, swap(): return lax.ppermute(x, 'entity', [(i, i ^ s) for i in range(shards)])  4.21 us
    ppermute x3, waiting for transfers between devices, swap(): return lax.ppermute(x, 'entity', [(i, i ^ s) for i in range(shards)])  1.78 us
    pallas_call x1, Pallas kernels, body(): call(prepare_kernel, [pltpu.SMEM] + [hbm] * 7, [out((total, 2 * total)),...  1.5 us
    pallas_call x1, Pallas kernels, body(): call(functools.partial(finish_kernel, width), [vmem] * 3, [out((width, sh...  1.09 us
    pallas_call x1, Pallas kernels, body(): call(lambda *refs: terms_kernel(buckets, negatives.shape[2], *refs), [vme...  0.92 us
    pallas_call x2, Pallas kernels, pick(): call(kernel, [vmem] * 3, [out((2 * cap, features), BF16)])  0.88 us
  transfers between devices with their start and end apart: 3, of which 1 were waited for; matrix products, arithmetic and copies ran while one was open for 0% of the time, Pallas kernels for 9%

profile of v5, /device:TPU:0, one launch (start us, length us, event | category | flops | bytes accessed | tf_op | source)
XLA Modules:
  0.0 24.8 jit_solution(3182900332178021209)
XLA Ops:
  0.6 0.5 %collective-permute-start = (bf16[1024,512]{1,0:T(8,128)(2,1)}, bf16[1024,512]{1,0:T(8,128)(2,1)S(1)}, u32[]{:S(2)}, u32[]{:S(2)}) collective-permute-start(bf16[1024,512]{1,0:T(8,128)(2,1)} %table_hbm.1), channel_id=1, source_target_pairs={{0,1},{1,0},{2,3},{3,2},{4,5},{5,4},{6,7},{7,6},{8,9},{9,8},{10,11... | collective-permute-start | bytes 3145736 | tf_op jit(solution)/shard_map/ppermute | solution.py:232
  1.2 2.6 %collective-permute-start.1 = (s32[1,4,16]{2,1,0:T(4,128)}, s32[1,4,16]{2,1,0:T(4,128)S(1)}, u32[]{:S(2)}, u32[]{:S(2)}) collective-permute-start(s32[1,4,16]{2,1,0:T(4,128)} %req_hbm.1), channel_id=1, source_target_pairs={{0,3},{1,2},{2,1},{3,0},{4,7},{5,6},{6,5},{7,4},{8,11},{9,10},{10,... | collective-permute-start | bytes 776 | tf_op jit(solution)/shard_map/ppermute | solution.py:232
  4.4 1.5 %shard_map.103 = (f32[64,128]{1,0:T(8,128)S(1)}, f32[64,128]{1,0:T(8,128)S(1)}, f32[4,4,128]{2,1,0:T(4,128)S(1)}, s32[1,4,16]{2,1,0:T(4,128)S(1)}, bf16[1024,512...) custom-call(s32[1]{0:T(128)S(6)} %copy.11.count_ref, s32[1,2,128]{2,1,0:T(2,128)} %head_hbm.1, ...), custom_call_target="tpu_custom_call" | custom-call | tf_op jit(solution)/shard_map/pallas_call | solution.py:243
  6.0 0.0 collective-permute-done.1.asked_ref
  6.0 0.0 collective-permute-done.other_ref
  6.0 0.4 %shard_map.106 = bf16[32,512]{1,0:T(8,128)(2,1)S(1)} custom-call(bf16[1024,512]{1,0:T(8,128)(2,1)S(1)} %get-tuple-element.21.near_ref, bf16[1024,512]{1,0:T(8,128)(2,1)S(1)} %collective-permute-done.other_ref, s32[1,4,16]{2,1,0:T(4,128)S(1)} %collective-permute-done.1.asked_ref), custom_call_target="tpu_custom_call" | custom-call | tf_op jit(solution)/shard_map/pallas_call | solution.py:264
  6.4 1.1 %collective-permute-start.2 = (bf16[32,512]{1,0:T(8,128)(2,1)S(1)}, bf16[32,512]{1,0:T(8,128)(2,1)S(1)}, u32[]{:S(2)}, u32[]{:S(2)}) collective-permute-start(bf16[32,512]{1,0:T(8,128)(2,1)S(1)} %shard_map.106), channel_id=1, source_target_pairs={{0,3},{1,2},{2,1},{3,0},{4,7},{5,6},{6,5},{7,4},{8,11},{9,10},{10,... | collective-permute-start | bytes 98312 | tf_op jit(solution)/shard_map/ppermute | solution.py:232
  7.5 0.2 shard_map.104.refs_1_
  7.7 0.4 %shard_map.105.refs_6_ = bf16[32,512]{1,0:T(8,128)(2,1)S(1)} custom-call(bf16[1024,512]{1,0:T(8,128)(2,1)S(1)} %get-tuple-element.21.near_ref, bf16[1024,512]{1,0:T(8,128)(2,1)S(1)} %collective-permute-done.other_ref, s32[1,4,16]{2,1,0:T(4,128)S(1)} %get-tuple-element.22.asked_ref), custom_call_target="tpu_custom_call" | custom-call | tf_op jit(solution)/shard_map/pallas_call | solution.py:264
  8.1 1.8 %collective-permute-done.2.refs_7_ = bf16[32,512]{1,0:T(8,128)(2,1)S(1)} collective-permute-done((bf16[32,512]{1,0:T(8,128)(2,1)S(1)}, bf16[32,512]{1,0:T(8,128)(2,1)S(1)}, u32[]{:S(2)}, u32[]{:S(2)}) %collective-permute-start.2) | collective-permute-done | bytes 32800 | tf_op jit(solution)/shard_map/ppermute | solution.py:232
  9.9 0.9 %shard_map.107 = (bf16[32,3,4,128]{3,2,1,0:T(4,128)(2,1)S(1)}, f32[512,512]{1,0:T(8,128)S(1)}, f32[1,512]{1,0:T(1,128)S(1)}) custom-call(bf16[1,512,512]{2,1,0:T(8,128)(2,1)S(1)} %get-tuple-element.16.panel_ref.refs_0_, bf16[512,512]{1,0:T(8,128)(2,1)S(1)} %shard_map.104.refs_1_, bf16[1,512]{1,0:T(2,128)(2,1)S(1)} %get-tuple-element.17.refs_2_, ...), custom_call_target="tpu_custom_call" | custom-call | tf_op jit(solution)/shard_map/pallas_call | solution.py:269
  10.8 12.9 %all_to_all.5.got_ref = bf16[32,3,4,128]{3,2,1,0:T(4,128)(2,1)S(1)} all-to-all(bf16[32,3,4,128]{3,2,1,0:T(4,128)(2,1)S(1)} %get-tuple-element.23), channel_id=1, replica_groups=mesh['bucket'=8,'entity'=4] {'bucket','entity'}, dimensions={0} | all-to-all | bytes 196608 | tf_op jit(solution)/shard_map/all_to_all | solution.py:274
  23.7 1.1 %shard_map.108 = (f32[64,1024]{1,0:T(8,128)}, f32[1,512,512]{2,1,0:T(8,128)}, f32[1,512]{1,0:T(1,128)}) custom-call(bf16[32,3,4,128]{3,2,1,0:T(4,128)(2,1)S(1)} %all_to_all.5.got_ref, f32[512,512]{1,0:T(8,128)S(1)} %get-tuple-element.24.panel_ref, f32[1,512]{1,0:T(1,128)S(1)} %get-tuple-element.25.rel_grad_ref), custom_call_target="tpu_custom_call" | custom-call | tf_op jit(solution)/shard_map/pallas_call | solution.py:275
Async XLA Ops:
  0.6 5.3 %collective-permute-start = (bf16[1024,512]{1,0:T(8,128)(2,1)}, bf16[1024,512]{1,0:T(8,128)(2,1)S(1)}, u32[]{:S(2)}, u32[]{:S(2)}) collective-permute-start(bf16[1024,512]{1,0:T(8,128)(2,1)} %table_hbm.1), channel_id=1, source_target_pairs={{0,1},{1,0},{2,3},{3,2},{4,5},{5,4},{6,7},{7,6},{8,9},{9,8},{10,11... | collective-permute-start | bytes 3145736 | tf_op jit(solution)/shard_map/ppermute | solution.py:232
  1.2 4.8 %collective-permute-start.1 = (s32[1,4,16]{2,1,0:T(4,128)}, s32[1,4,16]{2,1,0:T(4,128)S(1)}, u32[]{:S(2)}, u32[]{:S(2)}) collective-permute-start(s32[1,4,16]{2,1,0:T(4,128)} %req_hbm.1), channel_id=1, source_target_pairs={{0,3},{1,2},{2,1},{3,0},{4,7},{5,6},{6,5},{7,4},{8,11},{9,10},{10,... | collective-permute-start | bytes 776 | tf_op jit(solution)/shard_map/ppermute | solution.py:232
  6.4 3.5 %collective-permute-start.2 = (bf16[32,512]{1,0:T(8,128)(2,1)S(1)}, bf16[32,512]{1,0:T(8,128)(2,1)S(1)}, u32[]{:S(2)}, u32[]{:S(2)}) collective-permute-start(bf16[32,512]{1,0:T(8,128)(2,1)S(1)} %shard_map.106), channel_id=1, source_target_pairs={{0,3},{1,2},{2,1},{3,0},{4,7},{5,6},{6,5},{7,4},{8,11},{9,10},{10,... | collective-permute-start | bytes 98312 | tf_op jit(solution)/shard_map/ppermute | solution.py:232

commit v6 on v5

--- a/solution.py
+++ b/solution.py
@@ -121,7 +121,7 @@
     out_ref[...] = jnp.transpose(panel_ref[0])
 
 
-def terms_kernel(buckets, negs, *refs):
+def terms_kernel(buckets, negs, place, *refs):
     panel_ref, turned_ref, rel_ref, edges_ref, pairs_ref, rows_ref = refs[:6]
     send_ref, panel_grad_ref, rel_grad_ref = refs[-3:]
     fetched = jnp.concatenate([r[...] for r in refs[6:-3]], axis=0)
@@ -169,7 +169,7 @@
         piece = jnp.where(lane < LANES // 2, near, far).reshape(total // (2 * FOLD), 2 * FOLD, LANES)
         piece = piece[:, :FOLD].astype(BF16)
         for s in range(shards):
-            to = b * shards + jnp.bitwise_xor(me, s)
+            to = lax.rem((b * shards + jnp.bitwise_xor(me, s)) * place, devices)
             send_ref[to, :tiles] = piece[s * tiles : (s + 1) * tiles]
             send_ref[to, tiles] = rows[s]
     from_others = jnp.sum(jnp.where(left, rounded, 0.0), axis=1, keepdims=True) * proj_f
@@ -191,11 +191,15 @@
 
     def part(i):
         got = got_ref[pl.ds(i * step, step)].astype(F32)
-        turned = [jnp.transpose(got[:, k].reshape(step * FOLD, LANES)) for k in range(tiles + 1)]
-        starts = [(t, at) for t in turned[:tiles] for at in (0, LANES // 2)]
-        values = jnp.concatenate([t[at : at + width] for t, at in starts], axis=1).astype(BF16)
-        digits = [turned[tiles][k * span // 2 : k * span // 2 + 1] for k in range(4 * tiles)]
-        high, low = jnp.concatenate(digits[0::2], axis=1), jnp.concatenate(digits[1::2], axis=1)
+        flat = [got[:, k].reshape(step * FOLD, LANES) for k in range(tiles + 1)]
+        group = max(1, LANES // (step * FOLD))
+        turned = [jnp.transpose(jnp.concatenate(flat[k : k + group], axis=0)) for k in range(0, tiles, group)]
+        values = [t[at : at + width] for t in turned for at in (0, LANES // 2)]
+        values = jnp.concatenate(values, axis=1).astype(BF16)
+        digits = jnp.transpose(flat[tiles])
+        places = [2 * (k + g) + half for k in range(0, tiles, group) for half in (0, 1) for g in range(group)]
+        high = jnp.concatenate([digits[p * span : p * span + 1] for p in places], axis=1)
+        low = jnp.concatenate([digits[p * span + span // 2 : p * span + span // 2 + 1] for p in places], axis=1)
         hot = (low.astype(I32) == iota((DIGIT, low.shape[1]), 0)).astype(F32).astype(BF16)
         kept = [values * (high == float(h)).astype(F32).astype(BF16) for h in range(rows // DIGIT)]
         return dot(jnp.concatenate(kept, axis=0), hot, (1, 1))
@@ -265,13 +269,18 @@
 
     found = [pick(1, ids) for ids in asked]
     parts = [pick(0, own)] + [swap(x, 2 * c + 3) for c, x in enumerate(found)]
+    devices = buckets * shards
+    stride = devices - 5
+    order = [p * stride % devices for p in range(devices)]
     [turned] = call(turn_kernel, [vmem], [out((features, features), BF16)])(panel)
     send, panel_grad, rel_grad = call(
-        lambda *refs: terms_kernel(buckets, negatives.shape[2], *refs),
+        functools.partial(terms_kernel, buckets, negatives.shape[2], pow(stride, -1, devices)),
         [vmem] * (6 + len(parts)),
-        [out((buckets * shards, cap // (2 * FOLD) + 1, FOLD, LANES), BF16), out((features, features)), out((1, features))],
+        [out((devices, cap // (2 * FOLD) + 1, FOLD, LANES), BF16), out((features, features)), out((1, features))],
     )(panel, turned, rel, edges, pairs, rows, *parts)
-    got = lax.all_to_all(send, ("bucket", "entity"), split_axis=0, concat_axis=0, tiled=True)
+    got = lax.all_to_all(
+        send, ("bucket", "entity"), split_axis=0, concat_axis=0, tiled=True, axis_index_groups=[order]
+    )
     ent_grad, panel_grad, rel_grad = call(
         functools.partial(finish_kernel, width),
         [vmem] * 3,

time: 25 us -> 24.5 us (0.980)
  blocking collectives: 12.9 us -> 12.4 us
    all_to_all x1, blocking collectives: 12.9 us -> 12.4 us  [body(): lax.all_to_all(send, ('bucket', 'entity'), split_axis=0, concat_axis=0, t...]
where the time goes in v6:
time: 24.5 us; the launch traced here: 24.3 us
  blocking collectives  12.4 us (51%)
  Pallas kernels  4.57 us (19%)
  starting transfers between devices  4.21 us (17%)
  waiting for transfers between devices  1.78 us (7%)
  between operations  1.32 us (5%)
    all_to_all x1, blocking collectives, body(): lax.all_to_all(send, ('bucket', 'entity'), split_axis=0, concat_axis=0, t...  12.4 us
    ppermute x3, starting transfers between devices, swap(): return lax.ppermute(x, 'entity', [(i, i ^ s) for i in range(shards)])  4.21 us
    ppermute x3, waiting for transfers between devices, swap(): return lax.ppermute(x, 'entity', [(i, i ^ s) for i in range(shards)])  1.78 us
    pallas_call x1, Pallas kernels, body(): call(prepare_kernel, [pltpu.SMEM] + [hbm] * 7, [out((total, 2 * total)),...  1.5 us
    pallas_call x1, Pallas kernels, body(): call(functools.partial(finish_kernel, width), [vmem] * 3, [out((width, sh...  1.09 us
    pallas_call x1, Pallas kernels, body(): call(functools.partial(terms_kernel, buckets, negatives.shape[2], pow(str...  0.92 us
    pallas_call x2, Pallas kernels, pick(): call(kernel, [vmem] * 3, [out((2 * cap, features), BF16)])  0.88 us
  transfers between devices with their start and end apart: 3, of which 1 were waited for; matrix products, arithmetic and copies ran while one was open for 0% of the time, Pallas kernels for 9%

profile of v6, /device:TPU:0, one launch (start us, length us, event | category | flops | bytes accessed | tf_op | source)
XLA Modules:
  0.0 24.3 jit_solution(13269292782471081963)
XLA Ops:
  0.6 0.5 %collective-permute-start = (bf16[1024,512]{1,0:T(8,128)(2,1)}, bf16[1024,512]{1,0:T(8,128)(2,1)S(1)}, u32[]{:S(2)}, u32[]{:S(2)}) collective-permute-start(bf16[1024,512]{1,0:T(8,128)(2,1)} %table_hbm.1), channel_id=1, source_target_pairs={{0,1},{1,0},{2,3},{3,2},{4,5},{5,4},{6,7},{7,6},{8,9},{9,8},{10,11... | collective-permute-start | bytes 3145736 | tf_op jit(solution)/shard_map/ppermute | solution.py:236
  1.2 2.6 %collective-permute-start.1 = (s32[1,4,16]{2,1,0:T(4,128)}, s32[1,4,16]{2,1,0:T(4,128)S(1)}, u32[]{:S(2)}, u32[]{:S(2)}) collective-permute-start(s32[1,4,16]{2,1,0:T(4,128)} %req_hbm.1), channel_id=1, source_target_pairs={{0,3},{1,2},{2,1},{3,0},{4,7},{5,6},{6,5},{7,4},{8,11},{9,10},{10,... | collective-permute-start | bytes 776 | tf_op jit(solution)/shard_map/ppermute | solution.py:236
  4.4 1.5 %shard_map.103 = (f32[64,128]{1,0:T(8,128)S(1)}, f32[64,128]{1,0:T(8,128)S(1)}, f32[4,4,128]{2,1,0:T(4,128)S(1)}, s32[1,4,16]{2,1,0:T(4,128)S(1)}, bf16[1024,512...) custom-call(s32[1]{0:T(128)S(6)} %copy.11.count_ref, s32[1,2,128]{2,1,0:T(2,128)} %head_hbm.1, ...), custom_call_target="tpu_custom_call" | custom-call | tf_op jit(solution)/shard_map/pallas_call | solution.py:247
  6.0 0.0 collective-permute-done.1.asked_ref
  6.0 0.0 collective-permute-done.other_ref
  6.0 0.4 %shard_map.106 = bf16[32,512]{1,0:T(8,128)(2,1)S(1)} custom-call(bf16[1024,512]{1,0:T(8,128)(2,1)S(1)} %get-tuple-element.21.near_ref, bf16[1024,512]{1,0:T(8,128)(2,1)S(1)} %collective-permute-done.other_ref, s32[1,4,16]{2,1,0:T(4,128)S(1)} %collective-permute-done.1.asked_ref), custom_call_target="tpu_custom_call" | custom-call | tf_op jit(solution)/shard_map/pallas_call | solution.py:268
  6.4 1.1 %collective-permute-start.2 = (bf16[32,512]{1,0:T(8,128)(2,1)S(1)}, bf16[32,512]{1,0:T(8,128)(2,1)S(1)}, u32[]{:S(2)}, u32[]{:S(2)}) collective-permute-start(bf16[32,512]{1,0:T(8,128)(2,1)S(1)} %shard_map.106), channel_id=1, source_target_pairs={{0,3},{1,2},{2,1},{3,0},{4,7},{5,6},{6,5},{7,4},{8,11},{9,10},{10,... | collective-permute-start | bytes 98312 | tf_op jit(solution)/shard_map/ppermute | solution.py:236
  7.5 0.2 shard_map.104.refs_1_
  7.7 0.4 %shard_map.105.refs_6_ = bf16[32,512]{1,0:T(8,128)(2,1)S(1)} custom-call(bf16[1024,512]{1,0:T(8,128)(2,1)S(1)} %get-tuple-element.21.near_ref, bf16[1024,512]{1,0:T(8,128)(2,1)S(1)} %collective-permute-done.other_ref, s32[1,4,16]{2,1,0:T(4,128)S(1)} %get-tuple-element.22.asked_ref), custom_call_target="tpu_custom_call" | custom-call | tf_op jit(solution)/shard_map/pallas_call | solution.py:268
  8.1 1.8 %collective-permute-done.2.refs_7_ = bf16[32,512]{1,0:T(8,128)(2,1)S(1)} collective-permute-done((bf16[32,512]{1,0:T(8,128)(2,1)S(1)}, bf16[32,512]{1,0:T(8,128)(2,1)S(1)}, u32[]{:S(2)}, u32[]{:S(2)}) %collective-permute-start.2) | collective-permute-done | bytes 32800 | tf_op jit(solution)/shard_map/ppermute | solution.py:236
  9.9 0.9 %shard_map.107 = (bf16[32,3,4,128]{3,2,1,0:T(4,128)(2,1)S(1)}, f32[512,512]{1,0:T(8,128)S(1)}, f32[1,512]{1,0:T(1,128)S(1)}) custom-call(bf16[1,512,512]{2,1,0:T(8,128)(2,1)S(1)} %get-tuple-element.16.panel_ref.refs_0_, bf16[512,512]{1,0:T(8,128)(2,1)S(1)} %shard_map.104.refs_1_, bf16[1,512]{1,0:T(2,128)(2,1)S(1)} %get-tuple-element.17.refs_2_, ...), custom_call_target="tpu_custom_call" | custom-call | tf_op jit(solution)/shard_map/pallas_call | solution.py:276
  10.8 12.4 %all_to_all.5.got_ref = bf16[32,3,4,128]{3,2,1,0:T(4,128)(2,1)S(1)} all-to-all(bf16[32,3,4,128]{3,2,1,0:T(4,128)(2,1)S(1)} %get-tuple-element.23), channel_id=1, replica_groups={{0,27,22,17,12,7,2,29,24,19,14,9,4,31,26,21,16,11,6,1,28,23,18,13,8,3,3..., dimensions={0} | all-to-all | bytes 196608 | tf_op jit(solution)/shard_map/all_to_all | solution.py:281
  23.2 1.1 %shard_map.108 = (f32[64,1024]{1,0:T(8,128)}, f32[1,512,512]{2,1,0:T(8,128)}, f32[1,512]{1,0:T(1,128)}) custom-call(bf16[32,3,4,128]{3,2,1,0:T(4,128)(2,1)S(1)} %all_to_all.5.got_ref, f32[512,512]{1,0:T(8,128)S(1)} %get-tuple-element.24.panel_ref, f32[1,512]{1,0:T(1,128)S(1)} %get-tuple-element.25.rel_grad_ref), custom_call_target="tpu_custom_call" | custom-call | tf_op jit(solution)/shard_map/pallas_call | solution.py:284
Async XLA Ops:
  0.6 5.3 %collective-permute-start = (bf16[1024,512]{1,0:T(8,128)(2,1)}, bf16[1024,512]{1,0:T(8,128)(2,1)S(1)}, u32[]{:S(2)}, u32[]{:S(2)}) collective-permute-start(bf16[1024,512]{1,0:T(8,128)(2,1)} %table_hbm.1), channel_id=1, source_target_pairs={{0,1},{1,0},{2,3},{3,2},{4,5},{5,4},{6,7},{7,6},{8,9},{9,8},{10,11... | collective-permute-start | bytes 3145736 | tf_op jit(solution)/shard_map/ppermute | solution.py:236
  1.2 4.8 %collective-permute-start.1 = (s32[1,4,16]{2,1,0:T(4,128)}, s32[1,4,16]{2,1,0:T(4,128)S(1)}, u32[]{:S(2)}, u32[]{:S(2)}) collective-permute-start(s32[1,4,16]{2,1,0:T(4,128)} %req_hbm.1), channel_id=1, source_target_pairs={{0,3},{1,2},{2,1},{3,0},{4,7},{5,6},{6,5},{7,4},{8,11},{9,10},{10,... | collective-permute-start | bytes 776 | tf_op jit(solution)/shard_map/ppermute | solution.py:236
  6.4 3.5 %collective-permute-start.2 = (bf16[32,512]{1,0:T(8,128)(2,1)S(1)}, bf16[32,512]{1,0:T(8,128)(2,1)S(1)}, u32[]{:S(2)}, u32[]{:S(2)}) collective-permute-start(bf16[32,512]{1,0:T(8,128)(2,1)S(1)} %shard_map.106), channel_id=1, source_target_pairs={{0,3},{1,2},{2,1},{3,0},{4,7},{5,6},{6,5},{7,4},{8,11},{9,10},{10,... | collective-permute-start | bytes 98312 | tf_op jit(solution)/shard_map/ppermute | solution.py:236

commit v7 on v6

--- a/solution.py
+++ b/solution.py
@@ -23,13 +23,6 @@
 
 def iota(shape, axis):
     return lax.broadcasted_iota(I32, shape, axis)
-
-
-def to_column(row_blocks):
-    k = row_blocks[0].shape[1]
-    tall = jnp.concatenate([jnp.broadcast_to(r, (k, k)) for r in row_blocks], axis=0)
-    pick = lax.rem(iota(tall.shape, 0), k) == iota(tall.shape, 1)
-    return jnp.sum(jnp.where(pick, tall, 0).astype(F32), axis=1, keepdims=True)
 
 
 def flip(column):
@@ -111,10 +104,10 @@
     me = lax.axis_index("entity")
     cap = asked_ref.shape[2]
     for k, table_ref in enumerate((near_ref, other_ref)):
-        column = to_column([asked_ref[0, pl.ds(jnp.bitwise_xor(me, k), 1), :]]).astype(I32)
-        hot = (column == iota((cap, table_ref.shape[0]), 1)).astype(F32).astype(BF16)
+        asked = asked_ref[0, pl.ds(jnp.bitwise_xor(me, k), 1), :]
+        hot = (asked == iota((table_ref.shape[0], cap), 0)).astype(F32).astype(BF16)
         at = (first ^ k) * cap
-        out_ref[at : at + cap] = dot(hot, table_ref[...], (1, 0)).astype(BF16)
+        out_ref[at : at + cap] = dot(hot, table_ref[...], (0, 0)).astype(BF16)
 
 
 def turn_kernel(panel_ref, out_ref):

time: 24.5 us -> 24.4 us (level)
  no operation moved by 1% of the time
where the time goes in v7:
time: 24.4 us; the launch traced here: 24.2 us
  blocking collectives  12.4 us (51%)
  Pallas kernels  4.51 us (18%)
  starting transfers between devices  4.22 us (17%)
  waiting for transfers between devices  1.81 us (7%)
  between operations  1.32 us (5%)
    all_to_all x1, blocking collectives, body(): lax.all_to_all(send, ('bucket', 'entity'), split_axis=0, concat_axis=0, t...  12.4 us
    ppermute x3, starting transfers between devices, swap(): return lax.ppermute(x, 'entity', [(i, i ^ s) for i in range(shards)])  4.22 us
    ppermute x3, waiting for transfers between devices, swap(): return lax.ppermute(x, 'entity', [(i, i ^ s) for i in range(shards)])  1.81 us
    pallas_call x1, Pallas kernels, body(): call(prepare_kernel, [pltpu.SMEM] + [hbm] * 7, [out((total, 2 * total)),...  1.5 us
    pallas_call x1, Pallas kernels, body(): call(functools.partial(finish_kernel, width), [vmem] * 3, [out((width, sh...  1.09 us
    pallas_call x1, Pallas kernels, body(): call(functools.partial(terms_kernel, buckets, negatives.shape[2], pow(str...  0.92 us
    pallas_call x2, Pallas kernels, pick(): call(kernel, [vmem] * 3, [out((2 * cap, features), BF16)])  0.81 us
  transfers between devices with their start and end apart: 3, of which 1 were waited for; matrix products, arithmetic and copies ran while one was open for 0% of the time, Pallas kernels for 9%

profile of v7, /device:TPU:0, one launch (start us, length us, event | category | flops | bytes accessed | tf_op | source)
XLA Modules:
  0.0 24.2 jit_solution(918024739845937572)
XLA Ops:
  0.6 0.5 %collective-permute-start = (bf16[1024,512]{1,0:T(8,128)(2,1)}, bf16[1024,512]{1,0:T(8,128)(2,1)S(1)}, u32[]{:S(2)}, u32[]{:S(2)}) collective-permute-start(bf16[1024,512]{1,0:T(8,128)(2,1)} %table_hbm.1), channel_id=1, source_target_pairs={{0,1},{1,0},{2,3},{3,2},{4,5},{5,4},{6,7},{7,6},{8,9},{9,8},{10,11... | collective-permute-start | bytes 3145736 | tf_op jit(solution)/shard_map/ppermute | solution.py:229
  1.2 2.6 %collective-permute-start.1 = (s32[1,4,16]{2,1,0:T(4,128)}, s32[1,4,16]{2,1,0:T(4,128)S(1)}, u32[]{:S(2)}, u32[]{:S(2)}) collective-permute-start(s32[1,4,16]{2,1,0:T(4,128)} %req_hbm.1), channel_id=1, source_target_pairs={{0,3},{1,2},{2,1},{3,0},{4,7},{5,6},{6,5},{7,4},{8,11},{9,10},{10,... | collective-permute-start | bytes 776 | tf_op jit(solution)/shard_map/ppermute | solution.py:229
  4.4 1.5 %shard_map.103 = (f32[64,128]{1,0:T(8,128)S(1)}, f32[64,128]{1,0:T(8,128)S(1)}, f32[4,4,128]{2,1,0:T(4,128)S(1)}, s32[1,4,16]{2,1,0:T(4,128)S(1)}, bf16[1024,512...) custom-call(s32[1]{0:T(128)S(6)} %copy.11.count_ref, s32[1,2,128]{2,1,0:T(2,128)} %head_hbm.1, ...), custom_call_target="tpu_custom_call" | custom-call | tf_op jit(solution)/shard_map/pallas_call | solution.py:240
  6.0 0.0 collective-permute-done.1.asked_ref
  6.0 0.0 collective-permute-done.other_ref
  6.0 0.4 %shard_map.106 = bf16[32,512]{1,0:T(8,128)(2,1)S(1)} custom-call(bf16[1024,512]{1,0:T(8,128)(2,1)S(1)} %get-tuple-element.21.near_ref, bf16[1024,512]{1,0:T(8,128)(2,1)S(1)} %collective-permute-done.other_ref, s32[1,4,16]{2,1,0:T(4,128)S(1)} %collective-permute-done.1.asked_ref), custom_call_target="tpu_custom_call" | custom-call | tf_op jit(solution)/shard_map/pallas_call | solution.py:261
  6.4 1.1 %collective-permute-start.2 = (bf16[32,512]{1,0:T(8,128)(2,1)S(1)}, bf16[32,512]{1,0:T(8,128)(2,1)S(1)}, u32[]{:S(2)}, u32[]{:S(2)}) collective-permute-start(bf16[32,512]{1,0:T(8,128)(2,1)S(1)} %shard_map.106), channel_id=1, source_target_pairs={{0,3},{1,2},{2,1},{3,0},{4,7},{5,6},{6,5},{7,4},{8,11},{9,10},{10,... | collective-permute-start | bytes 98312 | tf_op jit(solution)/shard_map/ppermute | solution.py:229
  7.4 0.2 shard_map.104.refs_1_
  7.6 0.4 %shard_map.105.refs_6_ = bf16[32,512]{1,0:T(8,128)(2,1)S(1)} custom-call(bf16[1024,512]{1,0:T(8,128)(2,1)S(1)} %get-tuple-element.21.near_ref, bf16[1024,512]{1,0:T(8,128)(2,1)S(1)} %collective-permute-done.other_ref, s32[1,4,16]{2,1,0:T(4,128)S(1)} %get-tuple-element.22.asked_ref), custom_call_target="tpu_custom_call" | custom-call | tf_op jit(solution)/shard_map/pallas_call | solution.py:261
  8.0 1.8 %collective-permute-done.2.refs_7_ = bf16[32,512]{1,0:T(8,128)(2,1)S(1)} collective-permute-done((bf16[32,512]{1,0:T(8,128)(2,1)S(1)}, bf16[32,512]{1,0:T(8,128)(2,1)S(1)}, u32[]{:S(2)}, u32[]{:S(2)}) %collective-permute-start.2) | collective-permute-done | bytes 32800 | tf_op jit(solution)/shard_map/ppermute | solution.py:229
  9.8 0.9 %shard_map.107 = (bf16[32,3,4,128]{3,2,1,0:T(4,128)(2,1)S(1)}, f32[512,512]{1,0:T(8,128)S(1)}, f32[1,512]{1,0:T(1,128)S(1)}) custom-call(bf16[1,512,512]{2,1,0:T(8,128)(2,1)S(1)} %get-tuple-element.16.panel_ref.refs_0_, bf16[512,512]{1,0:T(8,128)(2,1)S(1)} %shard_map.104.refs_1_, bf16[1,512]{1,0:T(2,128)(2,1)S(1)} %get-tuple-element.17.refs_2_, ...), custom_call_target="tpu_custom_call" | custom-call | tf_op jit(solution)/shard_map/pallas_call | solution.py:269
  10.8 12.4 %all_to_all.5.got_ref = bf16[32,3,4,128]{3,2,1,0:T(4,128)(2,1)S(1)} all-to-all(bf16[32,3,4,128]{3,2,1,0:T(4,128)(2,1)S(1)} %get-tuple-element.23), channel_id=1, replica_groups={{0,27,22,17,12,7,2,29,24,19,14,9,4,31,26,21,16,11,6,1,28,23,18,13,8,3,3..., dimensions={0} | all-to-all | bytes 196608 | tf_op jit(solution)/shard_map/all_to_all | solution.py:274
  23.1 1.1 %shard_map.108 = (f32[64,1024]{1,0:T(8,128)}, f32[1,512,512]{2,1,0:T(8,128)}, f32[1,512]{1,0:T(1,128)}) custom-call(bf16[32,3,4,128]{3,2,1,0:T(4,128)(2,1)S(1)} %all_to_all.5.got_ref, f32[512,512]{1,0:T(8,128)S(1)} %get-tuple-element.24.panel_ref, f32[1,512]{1,0:T(1,128)S(1)} %get-tuple-element.25.rel_grad_ref), custom_call_target="tpu_custom_call" | custom-call | tf_op jit(solution)/shard_map/pallas_call | solution.py:277
Async XLA Ops:
  0.6 5.3 %collective-permute-start = (bf16[1024,512]{1,0:T(8,128)(2,1)}, bf16[1024,512]{1,0:T(8,128)(2,1)S(1)}, u32[]{:S(2)}, u32[]{:S(2)}) collective-permute-start(bf16[1024,512]{1,0:T(8,128)(2,1)} %table_hbm.1), channel_id=1, source_target_pairs={{0,1},{1,0},{2,3},{3,2},{4,5},{5,4},{6,7},{7,6},{8,9},{9,8},{10,11... | collective-permute-start | bytes 3145736 | tf_op jit(solution)/shard_map/ppermute | solution.py:229
  1.2 4.8 %collective-permute-start.1 = (s32[1,4,16]{2,1,0:T(4,128)}, s32[1,4,16]{2,1,0:T(4,128)S(1)}, u32[]{:S(2)}, u32[]{:S(2)}) collective-permute-start(s32[1,4,16]{2,1,0:T(4,128)} %req_hbm.1), channel_id=1, source_target_pairs={{0,3},{1,2},{2,1},{3,0},{4,7},{5,6},{6,5},{7,4},{8,11},{9,10},{10,... | collective-permute-start | bytes 776 | tf_op jit(solution)/shard_map/ppermute | solution.py:229
  6.4 3.5 %collective-permute-start.2 = (bf16[32,512]{1,0:T(8,128)(2,1)S(1)}, bf16[32,512]{1,0:T(8,128)(2,1)S(1)}, u32[]{:S(2)}, u32[]{:S(2)}) collective-permute-start(bf16[32,512]{1,0:T(8,128)(2,1)S(1)} %shard_map.106), channel_id=1, source_target_pairs={{0,3},{1,2},{2,1},{3,0},{4,7},{5,6},{6,5},{7,4},{8,11},{9,10},{10,... | collective-permute-start | bytes 98312 | tf_op jit(solution)/shard_map/ppermute | solution.py:229

commit v8 on v7

--- a/solution.py
+++ b/solution.py
@@ -110,17 +110,25 @@
         out_ref[at : at + cap] = dot(hot, table_ref[...], (0, 0)).astype(BF16)
 
 
-def turn_kernel(panel_ref, out_ref):
-    out_ref[...] = jnp.transpose(panel_ref[0])
+def project(rows, turned, relation):
+    proj = dot(rows, turned, (1, 0)).astype(BF16)
+    return (proj.astype(F32) + relation.astype(F32)).astype(BF16), proj
+
+
+def near_kernel(panel_ref, rel_ref, rows_ref, turned_ref, centers_ref, proj_ref):
+    turned_ref[...] = jnp.transpose(panel_ref[0])
+    centers_ref[...], proj_ref[...] = project(rows_ref[...], turned_ref[...], rel_ref[...])
 
 
 def terms_kernel(buckets, negs, place, *refs):
-    panel_ref, turned_ref, rel_ref, edges_ref, pairs_ref, rows_ref = refs[:6]
+    panel_ref, turned_ref, rel_ref, edges_ref, pairs_ref, rows_ref, near_centers, near_proj = refs[:8]
     send_ref, panel_grad_ref, rel_grad_ref = refs[-3:]
-    fetched = jnp.concatenate([r[...] for r in refs[6:-3]], axis=0)
-    proj = dot(fetched, turned_ref[...], (1, 0)).astype(BF16)
+    parts = refs[8:-3]
+    fetched = jnp.concatenate([r[...] for r in parts], axis=0)
+    far_centers, far_proj = project(fetched[near_proj.shape[0] :], turned_ref[...], rel_ref[...])
+    proj = jnp.concatenate([near_proj[...], far_proj], axis=0)
+    centers = jnp.concatenate([near_centers[...], far_centers], axis=0)
     proj_f = proj.astype(F32)
-    centers = (proj_f + rel_ref[...].astype(F32)).astype(BF16)
     center_f = centers.astype(F32)
     total, features = proj.shape
     points = jnp.concatenate([centers, proj], axis=0)
@@ -265,12 +273,16 @@
     devices = buckets * shards
     stride = devices - 5
     order = [p * stride % devices for p in range(devices)]
-    [turned] = call(turn_kernel, [vmem], [out((features, features), BF16)])(panel)
+    turned, near_centers, near_proj = call(
+        near_kernel,
+        [vmem] * 3,
+        [out((features, features), BF16), out((2 * cap, features), BF16), out((2 * cap, features), BF16)],
+    )(panel, rel, parts[0])
     send, panel_grad, rel_grad = call(
         functools.partial(terms_kernel, buckets, negatives.shape[2], pow(stride, -1, devices)),
-        [vmem] * (6 + len(parts)),
+        [vmem] * (8 + len(parts)),
         [out((devices, cap // (2 * FOLD) + 1, FOLD, LANES), BF16), out((features, features)), out((1, features))],
-    )(panel, turned, rel, edges, pairs, rows, *parts)
+    )(panel, turned, rel, edges, pairs, rows, near_centers, near_proj, *parts)
     got = lax.all_to_all(
         send, ("bucket", "entity"), split_axis=0, concat_axis=0, tiled=True, axis_index_groups=[order]
     )

time: 24.4 us -> 24.4 us (level)
  no operation moved by 1% of the time
where the time goes in v8:
time: 24.4 us; the launch traced here: 24.2 us
  blocking collectives  12.4 us (51%)
  Pallas kernels  4.61 us (19%)
  starting transfers between devices  4.22 us (17%)
  waiting for transfers between devices  1.67 us (7%)
  between operations  1.32 us (5%)
    all_to_all x1, blocking collectives, body(): lax.all_to_all(send, ('bucket', 'entity'), split_axis=0, concat_axis=0, t...  12.4 us
    ppermute x3, starting transfers between devices, swap(): return lax.ppermute(x, 'entity', [(i, i ^ s) for i in range(shards)])  4.22 us
    ppermute x3, waiting for transfers between devices, swap(): return lax.ppermute(x, 'entity', [(i, i ^ s) for i in range(shards)])  1.67 us
    pallas_call x1, Pallas kernels, body(): call(prepare_kernel, [pltpu.SMEM] + [hbm] * 7, [out((total, 2 * total)),...  1.5 us
    pallas_call x1, Pallas kernels, body(): call(functools.partial(finish_kernel, width), [vmem] * 3, [out((width, sh...  1.09 us
    pallas_call x1, Pallas kernels, body(): call(functools.partial(terms_kernel, buckets, negatives.shape[2], pow(str...  0.88 us
    pallas_call x2, Pallas kernels, pick(): call(kernel, [vmem] * 3, [out((2 * cap, features), BF16)])  0.81 us
  transfers between devices with their start and end apart: 3, of which 1 were waited for; matrix products, arithmetic and copies ran while one was open for 0% of the time, Pallas kernels for 9%

profile of v8, /device:TPU:0, one launch (start us, length us, event | category | flops | bytes accessed | tf_op | source)
XLA Modules:
  0.0 24.2 jit_solution(1915175817903563114)
XLA Ops:
  0.6 0.5 %collective-permute-start = (bf16[1024,512]{1,0:T(8,128)(2,1)}, bf16[1024,512]{1,0:T(8,128)(2,1)S(1)}, u32[]{:S(2)}, u32[]{:S(2)}) collective-permute-start(bf16[1024,512]{1,0:T(8,128)(2,1)} %table_hbm.1), channel_id=1, source_target_pairs={{0,1},{1,0},{2,3},{3,2},{4,5},{5,4},{6,7},{7,6},{8,9},{9,8},{10,11... | collective-permute-start | bytes 3145736 | tf_op jit(solution)/shard_map/ppermute | solution.py:237
  1.2 2.6 %collective-permute-start.1 = (s32[1,4,16]{2,1,0:T(4,128)}, s32[1,4,16]{2,1,0:T(4,128)S(1)}, u32[]{:S(2)}, u32[]{:S(2)}) collective-permute-start(s32[1,4,16]{2,1,0:T(4,128)} %req_hbm.1), channel_id=1, source_target_pairs={{0,3},{1,2},{2,1},{3,0},{4,7},{5,6},{6,5},{7,4},{8,11},{9,10},{10,... | collective-permute-start | bytes 776 | tf_op jit(solution)/shard_map/ppermute | solution.py:237
  4.4 1.5 %shard_map.103 = (f32[64,128]{1,0:T(8,128)S(1)}, f32[64,128]{1,0:T(8,128)S(1)}, f32[4,4,128]{2,1,0:T(4,128)S(1)}, s32[1,4,16]{2,1,0:T(4,128)S(1)}, bf16[1024,512...) custom-call(s32[1]{0:T(128)S(6)} %copy.11.count_ref, s32[1,2,128]{2,1,0:T(2,128)} %head_hbm.1, ...), custom_call_target="tpu_custom_call" | custom-call | tf_op jit(solution)/shard_map/pallas_call | solution.py:248
  6.0 0.0 collective-permute-done.1.asked_ref
  6.0 0.0 collective-permute-done.other_ref
  6.0 0.4 %shard_map.106 = bf16[32,512]{1,0:T(8,128)(2,1)S(1)} custom-call(bf16[1024,512]{1,0:T(8,128)(2,1)S(1)} %get-tuple-element.21.near_ref, bf16[1024,512]{1,0:T(8,128)(2,1)S(1)} %collective-permute-done.other_ref, s32[1,4,16]{2,1,0:T(4,128)S(1)} %collective-permute-done.1.asked_ref), custom_call_target="tpu_custom_call" | custom-call | tf_op jit(solution)/shard_map/pallas_call | solution.py:269
  6.4 1.1 %collective-permute-start.2 = (bf16[32,512]{1,0:T(8,128)(2,1)S(1)}, bf16[32,512]{1,0:T(8,128)(2,1)S(1)}, u32[]{:S(2)}, u32[]{:S(2)}) collective-permute-start(bf16[32,512]{1,0:T(8,128)(2,1)S(1)} %shard_map.106), channel_id=1, source_target_pairs={{0,3},{1,2},{2,1},{3,0},{4,7},{5,6},{6,5},{7,4},{8,11},{9,10},{10,... | collective-permute-start | bytes 98312 | tf_op jit(solution)/shard_map/ppermute | solution.py:237
  7.4 0.4 %shard_map.104.rows_ref.refs_8_ = bf16[32,512]{1,0:T(8,128)(2,1)S(1)} custom-call(bf16[1024,512]{1,0:T(8,128)(2,1)S(1)} %get-tuple-element.21.near_ref, bf16[1024,512]{1,0:T(8,128)(2,1)S(1)} %collective-permute-done.other_ref, s32[1,4,16]{2,1,0:T(4,128)S(1)} %get-tuple-element.22.asked_ref), custom_call_target="tpu_custom_call" | custom-call | tf_op jit(solution)/shard_map/pallas_call | solution.py:269
  7.8 0.3 %shard_map.105 = (bf16[512,512]{1,0:T(8,128)(2,1)S(1)}, bf16[32,512]{1,0:T(8,128)(2,1)S(1)}, bf16[32,512]{1,0:T(8,128)(2,1)S(1)}) custom-call(bf16[1,512,512]{2,1,0:T(8,128)(2,1)S(1)} %get-tuple-element.19.panel_ref.refs_0_, bf16[1,512]{1,0:T(2,128)(2,1)S(1)} %get-tuple-element.20.rel_ref.refs_2_, bf16[32,512]{1,0:T(8,128)(2,1)S(1)} %shard_map.104.rows_ref.refs_8_), custom_call_target="tpu_custom_call" | custom-call | tf_op jit(solution)/shard_map/pallas_call | solution.py:276
  8.2 1.7 %collective-permute-done.2.refs_9_ = bf16[32,512]{1,0:T(8,128)(2,1)S(1)} collective-permute-done((bf16[32,512]{1,0:T(8,128)(2,1)S(1)}, bf16[32,512]{1,0:T(8,128)(2,1)S(1)}, u32[]{:S(2)}, u32[]{:S(2)}) %collective-permute-start.2) | collective-permute-done | bytes 32800 | tf_op jit(solution)/shard_map/ppermute | solution.py:237
  9.8 0.9 %shard_map.107 = (bf16[32,3,4,128]{3,2,1,0:T(4,128)(2,1)S(1)}, f32[512,512]{1,0:T(8,128)S(1)}, f32[1,512]{1,0:T(1,128)S(1)}) custom-call(bf16[1,512,512]{2,1,0:T(8,128)(2,1)S(1)} %get-tuple-element.19.panel_ref.refs_0_, bf16[512,512]{1,0:T(8,128)(2,1)S(1)} %get-tuple-element.23.refs_1_, bf16[1,512]{1,0:T(2,128)(2,1)S(1)} %get-tuple-element.20.rel_ref.refs_2_, ...), custom_call_target="tpu_custom_call" | custom-call | tf_op jit(solution)/shard_map/pallas_call | solution.py:281
  10.7 12.4 %all_to_all.5.got_ref = bf16[32,3,4,128]{3,2,1,0:T(4,128)(2,1)S(1)} all-to-all(bf16[32,3,4,128]{3,2,1,0:T(4,128)(2,1)S(1)} %get-tuple-element.29), channel_id=1, replica_groups={{0,27,22,17,12,7,2,29,24,19,14,9,4,31,26,21,16,11,6,1,28,23,18,13,8,3,3..., dimensions={0} | all-to-all | bytes 196608 | tf_op jit(solution)/shard_map/all_to_all | solution.py:286
  23.1 1.1 %shard_map.108 = (f32[64,1024]{1,0:T(8,128)}, f32[1,512,512]{2,1,0:T(8,128)}, f32[1,512]{1,0:T(1,128)}) custom-call(bf16[32,3,4,128]{3,2,1,0:T(4,128)(2,1)S(1)} %all_to_all.5.got_ref, f32[512,512]{1,0:T(8,128)S(1)} %get-tuple-element.30.panel_ref, f32[1,512]{1,0:T(1,128)S(1)} %get-tuple-element.31.rel_grad_ref), custom_call_target="tpu_custom_call" | custom-call | tf_op jit(solution)/shard_map/pallas_call | solution.py:289
Async XLA Ops:
  0.6 5.3 %collective-permute-start = (bf16[1024,512]{1,0:T(8,128)(2,1)}, bf16[1024,512]{1,0:T(8,128)(2,1)S(1)}, u32[]{:S(2)}, u32[]{:S(2)}) collective-permute-start(bf16[1024,512]{1,0:T(8,128)(2,1)} %table_hbm.1), channel_id=1, source_target_pairs={{0,1},{1,0},{2,3},{3,2},{4,5},{5,4},{6,7},{7,6},{8,9},{9,8},{10,11... | collective-permute-start | bytes 3145736 | tf_op jit(solution)/shard_map/ppermute | solution.py:237
  1.2 4.8 %collective-permute-start.1 = (s32[1,4,16]{2,1,0:T(4,128)}, s32[1,4,16]{2,1,0:T(4,128)S(1)}, u32[]{:S(2)}, u32[]{:S(2)}) collective-permute-start(s32[1,4,16]{2,1,0:T(4,128)} %req_hbm.1), channel_id=1, source_target_pairs={{0,3},{1,2},{2,1},{3,0},{4,7},{5,6},{6,5},{7,4},{8,11},{9,10},{10,... | collective-permute-start | bytes 776 | tf_op jit(solution)/shard_map/ppermute | solution.py:237
  6.4 3.5 %collective-permute-start.2 = (bf16[32,512]{1,0:T(8,128)(2,1)S(1)}, bf16[32,512]{1,0:T(8,128)(2,1)S(1)}, u32[]{:S(2)}, u32[]{:S(2)}) collective-permute-start(bf16[32,512]{1,0:T(8,128)(2,1)S(1)} %shard_map.106), channel_id=1, source_target_pairs={{0,3},{1,2},{2,1},{3,0},{4,7},{5,6},{6,5},{7,4},{8,11},{9,10},{10,... | collective-permute-start | bytes 98312 | tf_op jit(solution)/shard_map/ppermute | solution.py:237

commit v9 on v8

--- a/solution.py
+++ b/solution.py
@@ -170,7 +170,7 @@
         piece = jnp.where(lane < LANES // 2, near, far).reshape(total // (2 * FOLD), 2 * FOLD, LANES)
         piece = piece[:, :FOLD].astype(BF16)
         for s in range(shards):
-            to = lax.rem((b * shards + jnp.bitwise_xor(me, s)) * place, devices)
+            to = lax.rem((b * shards + jnp.bitwise_xor(me, s ^ 1)) * place, devices)
             send_ref[to, :tiles] = piece[s * tiles : (s + 1) * tiles]
             send_ref[to, tiles] = rows[s]
     from_others = jnp.sum(jnp.where(left, rounded, 0.0), axis=1, keepdims=True) * proj_f
@@ -272,7 +272,7 @@
     parts = [pick(0, own)] + [swap(x, 2 * c + 3) for c, x in enumerate(found)]
     devices = buckets * shards
     stride = devices - 5
-    order = [p * stride % devices for p in range(devices)]
+    order = [p * stride % devices ^ 1 for p in range(devices)]
     turned, near_centers, near_proj = call(
         near_kernel,
         [vmem] * 3,

time: 24.4 us -> 24.4 us (level)
  no operation moved by 1% of the time
where the time goes in v9:
time: 24.4 us; the launch traced here: 24.2 us
  blocking collectives  12.4 us (51%)
  Pallas kernels  4.61 us (19%)
  starting transfers between devices  4.22 us (17%)
  waiting for transfers between devices  1.67 us (7%)
  between operations  1.32 us (5%)
    all_to_all x1, blocking collectives, body(): lax.all_to_all(send, ('bucket', 'entity'), split_axis=0, concat_axis=0, t...  12.4 us
    ppermute x3, starting transfers between devices, swap(): return lax.ppermute(x, 'entity', [(i, i ^ s) for i in range(shards)])  4.22 us
    ppermute x3, waiting for transfers between devices, swap(): return lax.ppermute(x, 'entity', [(i, i ^ s) for i in range(shards)])  1.67 us
    pallas_call x1, Pallas kernels, body(): call(prepare_kernel, [pltpu.SMEM] + [hbm] * 7, [out((total, 2 * total)),...  1.5 us
    pallas_call x1, Pallas kernels, body(): call(functools.partial(finish_kernel, width), [vmem] * 3, [out((width, sh...  1.09 us
    pallas_call x1, Pallas kernels, body(): call(functools.partial(terms_kernel, buckets, negatives.shape[2], pow(str...  0.89 us
    pallas_call x2, Pallas kernels, pick(): call(kernel, [vmem] * 3, [out((2 * cap, features), BF16)])  0.81 us
  transfers between devices with their start and end apart: 3, of which 1 were waited for; matrix products, arithmetic and copies ran while one was open for 0% of the time, Pallas kernels for 9%

profile of v9, /device:TPU:0, one launch (start us, length us, event | category | flops | bytes accessed | tf_op | source)
XLA Modules:
  0.0 24.2 jit_solution(13604519095429710034)
XLA Ops:
  0.6 0.5 %collective-permute-start = (bf16[1024,512]{1,0:T(8,128)(2,1)}, bf16[1024,512]{1,0:T(8,128)(2,1)S(1)}, u32[]{:S(2)}, u32[]{:S(2)}) collective-permute-start(bf16[1024,512]{1,0:T(8,128)(2,1)} %table_hbm.1), channel_id=1, source_target_pairs={{0,1},{1,0},{2,3},{3,2},{4,5},{5,4},{6,7},{7,6},{8,9},{9,8},{10,11... | collective-permute-start | bytes 3145736 | tf_op jit(solution)/shard_map/ppermute | solution.py:237
  1.2 2.6 %collective-permute-start.1 = (s32[1,4,16]{2,1,0:T(4,128)}, s32[1,4,16]{2,1,0:T(4,128)S(1)}, u32[]{:S(2)}, u32[]{:S(2)}) collective-permute-start(s32[1,4,16]{2,1,0:T(4,128)} %req_hbm.1), channel_id=1, source_target_pairs={{0,3},{1,2},{2,1},{3,0},{4,7},{5,6},{6,5},{7,4},{8,11},{9,10},{10,... | collective-permute-start | bytes 776 | tf_op jit(solution)/shard_map/ppermute | solution.py:237
  4.4 1.5 %shard_map.103 = (f32[64,128]{1,0:T(8,128)S(1)}, f32[64,128]{1,0:T(8,128)S(1)}, f32[4,4,128]{2,1,0:T(4,128)S(1)}, s32[1,4,16]{2,1,0:T(4,128)S(1)}, bf16[1024,512...) custom-call(s32[1]{0:T(128)S(6)} %copy.11.count_ref, s32[1,2,128]{2,1,0:T(2,128)} %head_hbm.1, ...), custom_call_target="tpu_custom_call" | custom-call | tf_op jit(solution)/shard_map/pallas_call | solution.py:248
  6.0 0.0 collective-permute-done.1.asked_ref
  6.0 0.0 collective-permute-done.other_ref
  6.0 0.4 %shard_map.106 = bf16[32,512]{1,0:T(8,128)(2,1)S(1)} custom-call(bf16[1024,512]{1,0:T(8,128)(2,1)S(1)} %get-tuple-element.21.near_ref, bf16[1024,512]{1,0:T(8,128)(2,1)S(1)} %collective-permute-done.other_ref, s32[1,4,16]{2,1,0:T(4,128)S(1)} %collective-permute-done.1.asked_ref), custom_call_target="tpu_custom_call" | custom-call | tf_op jit(solution)/shard_map/pallas_call | solution.py:269
  6.4 1.1 %collective-permute-start.2 = (bf16[32,512]{1,0:T(8,128)(2,1)S(1)}, bf16[32,512]{1,0:T(8,128)(2,1)S(1)}, u32[]{:S(2)}, u32[]{:S(2)}) collective-permute-start(bf16[32,512]{1,0:T(8,128)(2,1)S(1)} %shard_map.106), channel_id=1, source_target_pairs={{0,3},{1,2},{2,1},{3,0},{4,7},{5,6},{6,5},{7,4},{8,11},{9,10},{10,... | collective-permute-start | bytes 98312 | tf_op jit(solution)/shard_map/ppermute | solution.py:237
  7.4 0.4 %shard_map.104.rows_ref.refs_8_ = bf16[32,512]{1,0:T(8,128)(2,1)S(1)} custom-call(bf16[1024,512]{1,0:T(8,128)(2,1)S(1)} %get-tuple-element.21.near_ref, bf16[1024,512]{1,0:T(8,128)(2,1)S(1)} %collective-permute-done.other_ref, s32[1,4,16]{2,1,0:T(4,128)S(1)} %get-tuple-element.22.asked_ref), custom_call_target="tpu_custom_call" | custom-call | tf_op jit(solution)/shard_map/pallas_call | solution.py:269
  7.8 0.3 %shard_map.105 = (bf16[512,512]{1,0:T(8,128)(2,1)S(1)}, bf16[32,512]{1,0:T(8,128)(2,1)S(1)}, bf16[32,512]{1,0:T(8,128)(2,1)S(1)}) custom-call(bf16[1,512,512]{2,1,0:T(8,128)(2,1)S(1)} %get-tuple-element.19.panel_ref.refs_0_, bf16[1,512]{1,0:T(2,128)(2,1)S(1)} %get-tuple-element.20.rel_ref.refs_2_, bf16[32,512]{1,0:T(8,128)(2,1)S(1)} %shard_map.104.rows_ref.refs_8_), custom_call_target="tpu_custom_call" | custom-call | tf_op jit(solution)/shard_map/pallas_call | solution.py:276
  8.2 1.7 %collective-permute-done.2.refs_9_ = bf16[32,512]{1,0:T(8,128)(2,1)S(1)} collective-permute-done((bf16[32,512]{1,0:T(8,128)(2,1)S(1)}, bf16[32,512]{1,0:T(8,128)(2,1)S(1)}, u32[]{:S(2)}, u32[]{:S(2)}) %collective-permute-start.2) | collective-permute-done | bytes 32800 | tf_op jit(solution)/shard_map/ppermute | solution.py:237
  9.8 0.9 %shard_map.107 = (bf16[32,3,4,128]{3,2,1,0:T(4,128)(2,1)S(1)}, f32[512,512]{1,0:T(8,128)S(1)}, f32[1,512]{1,0:T(1,128)S(1)}) custom-call(bf16[1,512,512]{2,1,0:T(8,128)(2,1)S(1)} %get-tuple-element.19.panel_ref.refs_0_, bf16[512,512]{1,0:T(8,128)(2,1)S(1)} %get-tuple-element.23.refs_1_, bf16[1,512]{1,0:T(2,128)(2,1)S(1)} %get-tuple-element.20.rel_ref.refs_2_, ...), custom_call_target="tpu_custom_call" | custom-call | tf_op jit(solution)/shard_map/pallas_call | solution.py:281
  10.7 12.4 %all_to_all.5.got_ref = bf16[32,3,4,128]{3,2,1,0:T(4,128)(2,1)S(1)} all-to-all(bf16[32,3,4,128]{3,2,1,0:T(4,128)(2,1)S(1)} %get-tuple-element.29), channel_id=1, replica_groups={{1,26,23,16,13,6,3,28,25,18,15,8,5,30,27,20,17,10,7,0,29,22,19,12,9,2,3..., dimensions={0} | all-to-all | bytes 196608 | tf_op jit(solution)/shard_map/all_to_all | solution.py:286
  23.1 1.1 %shard_map.108 = (f32[64,1024]{1,0:T(8,128)}, f32[1,512,512]{2,1,0:T(8,128)}, f32[1,512]{1,0:T(1,128)}) custom-call(bf16[32,3,4,128]{3,2,1,0:T(4,128)(2,1)S(1)} %all_to_all.5.got_ref, f32[512,512]{1,0:T(8,128)S(1)} %get-tuple-element.30.panel_ref, f32[1,512]{1,0:T(1,128)S(1)} %get-tuple-element.31.rel_grad_ref), custom_call_target="tpu_custom_call" | custom-call | tf_op jit(solution)/shard_map/pallas_call | solution.py:289
Async XLA Ops:
  0.6 5.3 %collective-permute-start = (bf16[1024,512]{1,0:T(8,128)(2,1)}, bf16[1024,512]{1,0:T(8,128)(2,1)S(1)}, u32[]{:S(2)}, u32[]{:S(2)}) collective-permute-start(bf16[1024,512]{1,0:T(8,128)(2,1)} %table_hbm.1), channel_id=1, source_target_pairs={{0,1},{1,0},{2,3},{3,2},{4,5},{5,4},{6,7},{7,6},{8,9},{9,8},{10,11... | collective-permute-start | bytes 3145736 | tf_op jit(solution)/shard_map/ppermute | solution.py:237
  1.2 4.8 %collective-permute-start.1 = (s32[1,4,16]{2,1,0:T(4,128)}, s32[1,4,16]{2,1,0:T(4,128)S(1)}, u32[]{:S(2)}, u32[]{:S(2)}) collective-permute-start(s32[1,4,16]{2,1,0:T(4,128)} %req_hbm.1), channel_id=1, source_target_pairs={{0,3},{1,2},{2,1},{3,0},{4,7},{5,6},{6,5},{7,4},{8,11},{9,10},{10,... | collective-permute-start | bytes 776 | tf_op jit(solution)/shard_map/ppermute | solution.py:237
  6.4 3.5 %collective-permute-start.2 = (bf16[32,512]{1,0:T(8,128)(2,1)S(1)}, bf16[32,512]{1,0:T(8,128)(2,1)S(1)}, u32[]{:S(2)}, u32[]{:S(2)}) collective-permute-start(bf16[32,512]{1,0:T(8,128)(2,1)S(1)} %shard_map.106), channel_id=1, source_target_pairs={{0,3},{1,2},{2,1},{3,0},{4,7},{5,6},{6,5},{7,4},{8,11},{9,10},{10,... | collective-permute-start | bytes 98312 | tf_op jit(solution)/shard_map/ppermute | solution.py:237

commit v10 on v9

--- a/solution.py
+++ b/solution.py
@@ -10,6 +10,7 @@
 MARGIN = 2.0
 LANES = 128
 FOLD = 4
+COPIES = 2
 DIGIT = 256
 F32 = jnp.float32
 BF16 = jnp.bfloat16
@@ -178,10 +179,12 @@
 
 
 def finish_kernel(width, got_ref, panel_ref, rel_grad_ref, sums_hbm, panel_hbm, rel_hbm, out_ref, sems):
-    moves = [
-        pltpu.make_async_copy(panel_ref, panel_hbm.at[0], sems.at[0]),
-        pltpu.make_async_copy(rel_grad_ref, rel_hbm, sems.at[1]),
-    ]
+    def copies(source, target, first):
+        step = source.shape[0] // COPIES
+        at = [pl.ds(i * step, step) for i in range(COPIES)]
+        return [pltpu.make_async_copy(source.at[a], target.at[a], sems.at[first + i]) for i, a in enumerate(at)]
+
+    moves = copies(panel_ref, panel_hbm.at[0], 1) + [pltpu.make_async_copy(rel_grad_ref, rel_hbm, sems.at[0])]
     for move in moves:
         move.start()
     devices, tiles, _, _ = got_ref.shape
@@ -219,8 +222,10 @@
             return 0
 
         lax.fori_loop(1, devices // step, more, 0)
-    moves.append(pltpu.make_async_copy(out_ref, sums_hbm, sems.at[2]))
-    moves[-1].start()
+    last = copies(out_ref, sums_hbm, 1 + COPIES)
+    for move in last:
+        move.start()
+    moves += last
     for move in moves:
         move.wait()
 
@@ -292,7 +297,7 @@
         [out((width, shard_rows)), out((1, features, features)), out((1, features))],
         [
             pltpu.VMEM((width, shard_rows), F32),
-            pltpu.SemaphoreType.DMA((3,)),
+            pltpu.SemaphoreType.DMA((1 + 2 * COPIES,)),
         ],
         hbm,
     )(got, panel_grad, rel_grad)

time: 24.4 us -> 24.4 us (level)
  no operation moved by 1% of the time
where the time goes in v10:
time: 24.4 us; the launch traced here: 24.2 us
  blocking collectives  12.4 us (51%)
  Pallas kernels  4.62 us (19%)
  starting transfers between devices  4.22 us (17%)
  waiting for transfers between devices  1.67 us (7%)
  between operations  1.32 us (5%)
    all_to_all x1, blocking collectives, body(): lax.all_to_all(send, ('bucket', 'entity'), split_axis=0, concat_axis=0, t...  12.4 us
    ppermute x3, starting transfers between devices, swap(): return lax.ppermute(x, 'entity', [(i, i ^ s) for i in range(shards)])  4.22 us
    ppermute x3, waiting for transfers between devices, swap(): return lax.ppermute(x, 'entity', [(i, i ^ s) for i in range(shards)])  1.67 us
    pallas_call x1, Pallas kernels, body(): call(prepare_kernel, [pltpu.SMEM] + [hbm] * 7, [out((total, 2 * total)),...  1.5 us
    pallas_call x1, Pallas kernels, body(): call(functools.partial(finish_kernel, width), [vmem] * 3, [out((width, sh...  1.11 us
    pallas_call x1, Pallas kernels, body(): call(functools.partial(terms_kernel, buckets, negatives.shape[2], pow(str...  0.89 us
    pallas_call x2, Pallas kernels, pick(): call(kernel, [vmem] * 3, [out((2 * cap, features), BF16)])  0.81 us
  transfers between devices with their start and end apart: 3, of which 1 were waited for; matrix products, arithmetic and copies ran while one was open for 0% of the time, Pallas kernels for 9%

profile of v10, /device:TPU:0, one launch (start us, length us, event | category | flops | bytes accessed | tf_op | source)
XLA Modules:
  0.0 24.2 jit_solution(625402812002998897)
XLA Ops:
  0.6 0.5 %collective-permute-start = (bf16[1024,512]{1,0:T(8,128)(2,1)}, bf16[1024,512]{1,0:T(8,128)(2,1)S(1)}, u32[]{:S(2)}, u32[]{:S(2)}) collective-permute-start(bf16[1024,512]{1,0:T(8,128)(2,1)} %table_hbm.1), channel_id=1, source_target_pairs={{0,1},{1,0},{2,3},{3,2},{4,5},{5,4},{6,7},{7,6},{8,9},{9,8},{10,11... | collective-permute-start | bytes 3145736 | tf_op jit(solution)/shard_map/ppermute | solution.py:242
  1.2 2.6 %collective-permute-start.1 = (s32[1,4,16]{2,1,0:T(4,128)}, s32[1,4,16]{2,1,0:T(4,128)S(1)}, u32[]{:S(2)}, u32[]{:S(2)}) collective-permute-start(s32[1,4,16]{2,1,0:T(4,128)} %req_hbm.1), channel_id=1, source_target_pairs={{0,3},{1,2},{2,1},{3,0},{4,7},{5,6},{6,5},{7,4},{8,11},{9,10},{10,... | collective-permute-start | bytes 776 | tf_op jit(solution)/shard_map/ppermute | solution.py:242
  4.4 1.5 %shard_map.103 = (f32[64,128]{1,0:T(8,128)S(1)}, f32[64,128]{1,0:T(8,128)S(1)}, f32[4,4,128]{2,1,0:T(4,128)S(1)}, s32[1,4,16]{2,1,0:T(4,128)S(1)}, bf16[1024,512...) custom-call(s32[1]{0:T(128)S(6)} %copy.11.count_ref, s32[1,2,128]{2,1,0:T(2,128)} %head_hbm.1, ...), custom_call_target="tpu_custom_call" | custom-call | tf_op jit(solution)/shard_map/pallas_call | solution.py:253
  6.0 0.0 collective-permute-done.1.asked_ref
  6.0 0.0 collective-permute-done.other_ref
  6.0 0.4 %shard_map.106 = bf16[32,512]{1,0:T(8,128)(2,1)S(1)} custom-call(bf16[1024,512]{1,0:T(8,128)(2,1)S(1)} %get-tuple-element.21.near_ref, bf16[1024,512]{1,0:T(8,128)(2,1)S(1)} %collective-permute-done.other_ref, s32[1,4,16]{2,1,0:T(4,128)S(1)} %collective-permute-done.1.asked_ref), custom_call_target="tpu_custom_call" | custom-call | tf_op jit(solution)/shard_map/pallas_call | solution.py:274
  6.4 1.1 %collective-permute-start.2 = (bf16[32,512]{1,0:T(8,128)(2,1)S(1)}, bf16[32,512]{1,0:T(8,128)(2,1)S(1)}, u32[]{:S(2)}, u32[]{:S(2)}) collective-permute-start(bf16[32,512]{1,0:T(8,128)(2,1)S(1)} %shard_map.106), channel_id=1, source_target_pairs={{0,3},{1,2},{2,1},{3,0},{4,7},{5,6},{6,5},{7,4},{8,11},{9,10},{10,... | collective-permute-start | bytes 98312 | tf_op jit(solution)/shard_map/ppermute | solution.py:242
  7.4 0.4 %shard_map.104.rows_ref.refs_8_ = bf16[32,512]{1,0:T(8,128)(2,1)S(1)} custom-call(bf16[1024,512]{1,0:T(8,128)(2,1)S(1)} %get-tuple-element.21.near_ref, bf16[1024,512]{1,0:T(8,128)(2,1)S(1)} %collective-permute-done.other_ref, s32[1,4,16]{2,1,0:T(4,128)S(1)} %get-tuple-element.22.asked_ref), custom_call_target="tpu_custom_call" | custom-call | tf_op jit(solution)/shard_map/pallas_call | solution.py:274
  7.8 0.3 %shard_map.105 = (bf16[512,512]{1,0:T(8,128)(2,1)S(1)}, bf16[32,512]{1,0:T(8,128)(2,1)S(1)}, bf16[32,512]{1,0:T(8,128)(2,1)S(1)}) custom-call(bf16[1,512,512]{2,1,0:T(8,128)(2,1)S(1)} %get-tuple-element.19.panel_ref.refs_0_, bf16[1,512]{1,0:T(2,128)(2,1)S(1)} %get-tuple-element.20.rel_ref.refs_2_, bf16[32,512]{1,0:T(8,128)(2,1)S(1)} %shard_map.104.rows_ref.refs_8_), custom_call_target="tpu_custom_call" | custom-call | tf_op jit(solution)/shard_map/pallas_call | solution.py:281
  8.2 1.7 %collective-permute-done.2.refs_9_ = bf16[32,512]{1,0:T(8,128)(2,1)S(1)} collective-permute-done((bf16[32,512]{1,0:T(8,128)(2,1)S(1)}, bf16[32,512]{1,0:T(8,128)(2,1)S(1)}, u32[]{:S(2)}, u32[]{:S(2)}) %collective-permute-start.2) | collective-permute-done | bytes 32800 | tf_op jit(solution)/shard_map/ppermute | solution.py:242
  9.8 0.9 %shard_map.107 = (bf16[32,3,4,128]{3,2,1,0:T(4,128)(2,1)S(1)}, f32[512,512]{1,0:T(8,128)S(1)}, f32[1,512]{1,0:T(1,128)S(1)}) custom-call(bf16[1,512,512]{2,1,0:T(8,128)(2,1)S(1)} %get-tuple-element.19.panel_ref.refs_0_, bf16[512,512]{1,0:T(8,128)(2,1)S(1)} %get-tuple-element.23.refs_1_, bf16[1,512]{1,0:T(2,128)(2,1)S(1)} %get-tuple-element.20.rel_ref.refs_2_, ...), custom_call_target="tpu_custom_call" | custom-call | tf_op jit(solution)/shard_map/pallas_call | solution.py:286
  10.7 12.4 %all_to_all.5.got_ref = bf16[32,3,4,128]{3,2,1,0:T(4,128)(2,1)S(1)} all-to-all(bf16[32,3,4,128]{3,2,1,0:T(4,128)(2,1)S(1)} %get-tuple-element.29), channel_id=1, replica_groups={{1,26,23,16,13,6,3,28,25,18,15,8,5,30,27,20,17,10,7,0,29,22,19,12,9,2,3..., dimensions={0} | all-to-all | bytes 196608 | tf_op jit(solution)/shard_map/all_to_all | solution.py:291
  23.1 1.1 %shard_map.108 = (f32[64,1024]{1,0:T(8,128)}, f32[1,512,512]{2,1,0:T(8,128)}, f32[1,512]{1,0:T(1,128)}) custom-call(bf16[32,3,4,128]{3,2,1,0:T(4,128)(2,1)S(1)} %all_to_all.5.got_ref, f32[512,512]{1,0:T(8,128)S(1)} %get-tuple-element.30.panel_ref, f32[1,512]{1,0:T(1,128)S(1)} %get-tuple-element.31.rel_grad_ref), custom_call_target="tpu_custom_call" | custom-call | tf_op jit(solution)/shard_map/pallas_call | solution.py:294
Async XLA Ops:
  0.6 5.3 %collective-permute-start = (bf16[1024,512]{1,0:T(8,128)(2,1)}, bf16[1024,512]{1,0:T(8,128)(2,1)S(1)}, u32[]{:S(2)}, u32[]{:S(2)}) collective-permute-start(bf16[1024,512]{1,0:T(8,128)(2,1)} %table_hbm.1), channel_id=1, source_target_pairs={{0,1},{1,0},{2,3},{3,2},{4,5},{5,4},{6,7},{7,6},{8,9},{9,8},{10,11... | collective-permute-start | bytes 3145736 | tf_op jit(solution)/shard_map/ppermute | solution.py:242
  1.2 4.8 %collective-permute-start.1 = (s32[1,4,16]{2,1,0:T(4,128)}, s32[1,4,16]{2,1,0:T(4,128)S(1)}, u32[]{:S(2)}, u32[]{:S(2)}) collective-permute-start(s32[1,4,16]{2,1,0:T(4,128)} %req_hbm.1), channel_id=1, source_target_pairs={{0,3},{1,2},{2,1},{3,0},{4,7},{5,6},{6,5},{7,4},{8,11},{9,10},{10,... | collective-permute-start | bytes 776 | tf_op jit(solution)/shard_map/ppermute | solution.py:242
  6.4 3.5 %collective-permute-start.2 = (bf16[32,512]{1,0:T(8,128)(2,1)S(1)}, bf16[32,512]{1,0:T(8,128)(2,1)S(1)}, u32[]{:S(2)}, u32[]{:S(2)}) collective-permute-start(bf16[32,512]{1,0:T(8,128)(2,1)S(1)} %shard_map.106), channel_id=1, source_target_pairs={{0,3},{1,2},{2,1},{3,0},{4,7},{5,6},{6,5},{7,4},{8,11},{9,10},{10,... | collective-permute-start | bytes 98312 | tf_op jit(solution)/shard_map/ppermute | solution.py:242

commit v11 on v9

--- a/solution.py
+++ b/solution.py
@@ -9,7 +9,7 @@
 
 MARGIN = 2.0
 LANES = 128
-FOLD = 4
+FOLD = 2
 DIGIT = 256
 F32 = jnp.float32
 BF16 = jnp.bfloat16

time: 24.4 us -> 24.4 us (level)
  no operation moved by 1% of the time
where the time goes in v11:
time: 24.4 us; the launch traced here: 24.2 us
  blocking collectives  12.3 us (50%)
  Pallas kernels  4.68 us (19%)
  starting transfers between devices  4.22 us (17%)
  waiting for transfers between devices  1.67 us (7%)
  between operations  1.33 us (5%)
    all_to_all x1, blocking collectives, body(): lax.all_to_all(send, ('bucket', 'entity'), split_axis=0, concat_axis=0, t...  12.3 us
    ppermute x3, starting transfers between devices, swap(): return lax.ppermute(x, 'entity', [(i, i ^ s) for i in range(shards)])  4.22 us
    ppermute x3, waiting for transfers between devices, swap(): return lax.ppermute(x, 'entity', [(i, i ^ s) for i in range(shards)])  1.67 us
    pallas_call x1, Pallas kernels, body(): call(prepare_kernel, [pltpu.SMEM] + [hbm] * 7, [out((total, 2 * total)),...  1.5 us
    pallas_call x1, Pallas kernels, body(): call(functools.partial(finish_kernel, width), [vmem] * 3, [out((width, sh...  1.16 us
    pallas_call x1, Pallas kernels, body(): call(functools.partial(terms_kernel, buckets, negatives.shape[2], pow(str...  0.89 us
    pallas_call x2, Pallas kernels, pick(): call(kernel, [vmem] * 3, [out((2 * cap, features), BF16)])  0.81 us
  transfers between devices with their start and end apart: 3, of which 1 were waited for; matrix products, arithmetic and copies ran while one was open for 0% of the time, Pallas kernels for 9%

profile of v11, /device:TPU:0, one launch (start us, length us, event | category | flops | bytes accessed | tf_op | source)
XLA Modules:
  0.0 24.2 jit_solution(3537451345945903494)
XLA Ops:
  0.6 0.5 %collective-permute-start = (bf16[1024,512]{1,0:T(8,128)(2,1)}, bf16[1024,512]{1,0:T(8,128)(2,1)S(1)}, u32[]{:S(2)}, u32[]{:S(2)}) collective-permute-start(bf16[1024,512]{1,0:T(8,128)(2,1)} %table_hbm.1), channel_id=1, source_target_pairs={{0,1},{1,0},{2,3},{3,2},{4,5},{5,4},{6,7},{7,6},{8,9},{9,8},{10,11... | collective-permute-start | bytes 3145736 | tf_op jit(solution)/shard_map/ppermute | solution.py:237
  1.2 2.6 %collective-permute-start.1 = (s32[1,4,16]{2,1,0:T(4,128)}, s32[1,4,16]{2,1,0:T(4,128)S(1)}, u32[]{:S(2)}, u32[]{:S(2)}) collective-permute-start(s32[1,4,16]{2,1,0:T(4,128)} %req_hbm.1), channel_id=1, source_target_pairs={{0,3},{1,2},{2,1},{3,0},{4,7},{5,6},{6,5},{7,4},{8,11},{9,10},{10,... | collective-permute-start | bytes 776 | tf_op jit(solution)/shard_map/ppermute | solution.py:237
  4.4 1.5 %shard_map.103 = (f32[64,128]{1,0:T(8,128)S(1)}, f32[64,128]{1,0:T(8,128)S(1)}, f32[4,2,128]{2,1,0:T(2,128)S(1)}, s32[1,4,16]{2,1,0:T(4,128)S(1)}, bf16[1024,512...) custom-call(s32[1]{0:T(128)S(6)} %copy.11.count_ref, s32[1,2,128]{2,1,0:T(2,128)} %head_hbm.1, ...), custom_call_target="tpu_custom_call" | custom-call | tf_op jit(solution)/shard_map/pallas_call | solution.py:248
  6.0 0.0 collective-permute-done.1.asked_ref
  6.0 0.0 collective-permute-done.other_ref
  6.0 0.4 %shard_map.106 = bf16[32,512]{1,0:T(8,128)(2,1)S(1)} custom-call(bf16[1024,512]{1,0:T(8,128)(2,1)S(1)} %get-tuple-element.21.near_ref, bf16[1024,512]{1,0:T(8,128)(2,1)S(1)} %collective-permute-done.other_ref, s32[1,4,16]{2,1,0:T(4,128)S(1)} %collective-permute-done.1.asked_ref), custom_call_target="tpu_custom_call" | custom-call | tf_op jit(solution)/shard_map/pallas_call | solution.py:269
  6.4 1.1 %collective-permute-start.2 = (bf16[32,512]{1,0:T(8,128)(2,1)S(1)}, bf16[32,512]{1,0:T(8,128)(2,1)S(1)}, u32[]{:S(2)}, u32[]{:S(2)}) collective-permute-start(bf16[32,512]{1,0:T(8,128)(2,1)S(1)} %shard_map.106), channel_id=1, source_target_pairs={{0,3},{1,2},{2,1},{3,0},{4,7},{5,6},{6,5},{7,4},{8,11},{9,10},{10,... | collective-permute-start | bytes 98312 | tf_op jit(solution)/shard_map/ppermute | solution.py:237
  7.4 0.4 %shard_map.104.rows_ref.refs_8_ = bf16[32,512]{1,0:T(8,128)(2,1)S(1)} custom-call(bf16[1024,512]{1,0:T(8,128)(2,1)S(1)} %get-tuple-element.21.near_ref, bf16[1024,512]{1,0:T(8,128)(2,1)S(1)} %collective-permute-done.other_ref, s32[1,4,16]{2,1,0:T(4,128)S(1)} %get-tuple-element.22.asked_ref), custom_call_target="tpu_custom_call" | custom-call | tf_op jit(solution)/shard_map/pallas_call | solution.py:269
  7.8 0.3 %shard_map.105 = (bf16[512,512]{1,0:T(8,128)(2,1)S(1)}, bf16[32,512]{1,0:T(8,128)(2,1)S(1)}, bf16[32,512]{1,0:T(8,128)(2,1)S(1)}) custom-call(bf16[1,512,512]{2,1,0:T(8,128)(2,1)S(1)} %get-tuple-element.19.panel_ref.refs_0_, bf16[1,512]{1,0:T(2,128)(2,1)S(1)} %get-tuple-element.20.rel_ref.refs_2_, bf16[32,512]{1,0:T(8,128)(2,1)S(1)} %shard_map.104.rows_ref.refs_8_), custom_call_target="tpu_custom_call" | custom-call | tf_op jit(solution)/shard_map/pallas_call | solution.py:276
  8.2 1.7 %collective-permute-done.2.refs_9_ = bf16[32,512]{1,0:T(8,128)(2,1)S(1)} collective-permute-done((bf16[32,512]{1,0:T(8,128)(2,1)S(1)}, bf16[32,512]{1,0:T(8,128)(2,1)S(1)}, u32[]{:S(2)}, u32[]{:S(2)}) %collective-permute-start.2) | collective-permute-done | bytes 32800 | tf_op jit(solution)/shard_map/ppermute | solution.py:237
  9.8 0.9 %shard_map.107 = (bf16[32,5,2,128]{3,2,1,0:T(2,128)(2,1)S(1)}, f32[512,512]{1,0:T(8,128)S(1)}, f32[1,512]{1,0:T(1,128)S(1)}) custom-call(bf16[1,512,512]{2,1,0:T(8,128)(2,1)S(1)} %get-tuple-element.19.panel_ref.refs_0_, bf16[512,512]{1,0:T(8,128)(2,1)S(1)} %get-tuple-element.23.refs_1_, bf16[1,512]{1,0:T(2,128)(2,1)S(1)} %get-tuple-element.20.rel_ref.refs_2_, ...), custom_call_target="tpu_custom_call" | custom-call | tf_op jit(solution)/shard_map/pallas_call | solution.py:281
  10.7 12.3 %all_to_all.5.got_ref = bf16[32,5,2,128]{3,2,1,0:T(2,128)(2,1)S(1)} all-to-all(bf16[32,5,2,128]{3,2,1,0:T(2,128)(2,1)S(1)} %get-tuple-element.29), channel_id=1, replica_groups={{1,26,23,16,13,6,3,28,25,18,15,8,5,30,27,20,17,10,7,0,29,22,19,12,9,2,3..., dimensions={0} | all-to-all | bytes 163840 | tf_op jit(solution)/shard_map/all_to_all | solution.py:286
  23.1 1.2 %shard_map.108 = (f32[64,1024]{1,0:T(8,128)}, f32[1,512,512]{2,1,0:T(8,128)}, f32[1,512]{1,0:T(1,128)}) custom-call(bf16[32,5,2,128]{3,2,1,0:T(2,128)(2,1)S(1)} %all_to_all.5.got_ref, f32[512,512]{1,0:T(8,128)S(1)} %get-tuple-element.30.panel_ref, f32[1,512]{1,0:T(1,128)S(1)} %get-tuple-element.31.rel_grad_ref), custom_call_target="tpu_custom_call" | custom-call | tf_op jit(solution)/shard_map/pallas_call | solution.py:289
Async XLA Ops:
  0.6 5.3 %collective-permute-start = (bf16[1024,512]{1,0:T(8,128)(2,1)}, bf16[1024,512]{1,0:T(8,128)(2,1)S(1)}, u32[]{:S(2)}, u32[]{:S(2)}) collective-permute-start(bf16[1024,512]{1,0:T(8,128)(2,1)} %table_hbm.1), channel_id=1, source_target_pairs={{0,1},{1,0},{2,3},{3,2},{4,5},{5,4},{6,7},{7,6},{8,9},{9,8},{10,11... | collective-permute-start | bytes 3145736 | tf_op jit(solution)/shard_map/ppermute | solution.py:237
  1.2 4.8 %collective-permute-start.1 = (s32[1,4,16]{2,1,0:T(4,128)}, s32[1,4,16]{2,1,0:T(4,128)S(1)}, u32[]{:S(2)}, u32[]{:S(2)}) collective-permute-start(s32[1,4,16]{2,1,0:T(4,128)} %req_hbm.1), channel_id=1, source_target_pairs={{0,3},{1,2},{2,1},{3,0},{4,7},{5,6},{6,5},{7,4},{8,11},{9,10},{10,... | collective-permute-start | bytes 776 | tf_op jit(solution)/shard_map/ppermute | solution.py:237
  6.4 3.5 %collective-permute-start.2 = (bf16[32,512]{1,0:T(8,128)(2,1)S(1)}, bf16[32,512]{1,0:T(8,128)(2,1)S(1)}, u32[]{:S(2)}, u32[]{:S(2)}) collective-permute-start(bf16[32,512]{1,0:T(8,128)(2,1)S(1)} %shard_map.106), channel_id=1, source_target_pairs={{0,3},{1,2},{2,1},{3,0},{4,7},{5,6},{6,5},{7,4},{8,11},{9,10},{10,... | collective-permute-start | bytes 98312 | tf_op jit(solution)/shard_map/ppermute | solution.py:237
